TPU v7x, 256 devices: a whole 4x4x8 slice. The times are simulated.
256 devices in a mesh: seq: 128 (over z, y, x), head: 2 (over core).
Axes of the slice: x: 4, y: 4, z: 8, core: 2. Of those that a mesh axis runs over, the one named last changes fastest.
Arguments:
- query_vectors: bfloat16 [16384, 2048], P('seq', 'head'), may hold values from -12 to 12
- key_vectors: bfloat16 [16384, 2048], P('seq', 'head'), may hold values from -12 to 12
- value_vectors: bfloat16 [16384, 2048], P('seq', 'head'), may hold values from -6 to 6
- cotangent: bfloat16 [16384, 2048], P('seq', 'head'), may hold values from -24 to 24
- rand_peer: int32 [2, 256, 8, 3], P('head', 'seq'), may hold values from 0 to 127, all different within a row; in each aligned block of 16 rows (0 to 15, 16 to 31, ..., all dimensions but the last counted through in order) at most 2 rows name the same one
- rand_local: int32 [2, 256, 8, 3], P('head', 'seq'), may hold values from 0 to 1
- global_ids: int32 [2], replicated, may hold values from 0 to 255, as said below
Outputs:
- attended: bfloat16 [16384, 2048], P(('seq', 'head'))
- grad_query: bfloat16 [16384, 2048], P(('seq', 'head'))
- grad_key: bfloat16 [16384, 2048], P(('seq', 'head'))
- grad_value: bfloat16 [16384, 2048], P(('seq', 'head'))
Inputs may be any that keep to these rules, and one draw needn't show every extreme that they name: `rand_peer`: per head group, query block and head, three different numbers. Among the 48 entries of one index of seq and head, no number appears more than 2 times; in some such rows one appears exactly 2 times. `global_ids`: two different blocks; one of them, in either place, is the last block 255.
All inputs are finite; a program needn't handle non-finite values.
Results may differ from a plain program's by a relative error of at most 0.0065.
Values may be sent and summed in bfloat16 or wider, within the bound.
A program may use at most 128 MiB of HBM per device.

v0:
```python
import jax
import jax.numpy as jnp
from jax import lax
from jax.sharding import PartitionSpec as P

HEAD_DIM = 128
BLOCK = 64


def with_halo(cells, sides, width):
    for axis, dim in sides:
        count = lax.axis_size(axis)
        ends = count - 1
        head = lax.slice_in_dim(cells, 0, width, axis=dim)
        tail = lax.slice_in_dim(cells, cells.shape[dim] - width, cells.shape[dim], axis=dim)
        cells = jnp.concatenate(
            [
                lax.ppermute(tail, axis, [(i, (i + 1) % count) for i in range(ends)]),
                cells,
                lax.ppermute(head, axis, [((i + 1) % count, i) for i in range(ends)]),
            ],
            axis=dim,
        )
    return cells


def spread(value, axis, source):
    kept = jnp.where(lax.axis_index(axis) == source, value, 0).astype(value.dtype)
    return lax.psum(kept, axis)


def shifted(value, axis, steps):
    count = lax.axis_size(axis)
    initial, last = (max(0, -steps), min(count, count - steps))
    return lax.ppermute(value, axis, [(source, source + steps) for source in range(initial, last)])


def block_heads(source_array, head_count):
    token_count = source_array.shape[0]
    return source_array.reshape(token_count // BLOCK, BLOCK, head_count, HEAD_DIM).transpose(
        2, 0, 1, 3
    )


def token_rows(source_array):
    head_count, block_count, block_len, feature_count = source_array.shape
    return source_array.transpose(1, 2, 0, 3).reshape(
        block_count * block_len, head_count * feature_count
    )


def slot_numbers(peer_flat, slot_depth):
    pick_total = peer_flat.shape[0]
    positions = jnp.arange(pick_total, dtype=jnp.int32)
    same_peer = peer_flat[:, None] == peer_flat[None, :]
    earlier = positions[None, :] < positions[:, None]
    rank_in_peer = jnp.sum(jnp.logical_and(same_peer, earlier), axis=1)
    return peer_flat * slot_depth + rank_in_peer


def on_device(
    query_vectors, key_vectors, value_vectors, cotangent, rand_peer, rand_local, global_ids
):
    seq_count = lax.axis_size("seq")
    seq_index = lax.axis_index("seq")
    tokens_here = query_vectors.shape[0]
    head_count = query_vectors.shape[1] // HEAD_DIM
    blocks_here = tokens_here // BLOCK
    all_blocks = seq_count * blocks_here
    slot_depth = max(2, 3 * blocks_here * head_count // seq_count + 1)
    slot_total = seq_count * slot_depth
    pick_total = blocks_here * head_count * 3
    score_scale = HEAD_DIM ** (-0.5)
    key_value = jnp.stack([key_vectors, value_vectors])
    padded = with_halo(key_value, (("seq", 1),), BLOCK)
    padded_blocks = padded.reshape(2, blocks_here + 2, BLOCK, head_count, HEAD_DIM)
    windows = jnp.stack(
        [padded_blocks[:, offset : offset + blocks_here] for offset in range(3)], axis=2
    )
    windows = windows.transpose(4, 1, 2, 0, 3, 5)
    owners = global_ids // blocks_here
    spot_ids = global_ids % blocks_here
    own_blocks = key_value.reshape(2, blocks_here, BLOCK, head_count * HEAD_DIM)
    fetched = []
    for global_slot in range(2):
        own_piece = lax.dynamic_index_in_dim(own_blocks, spot_ids[global_slot], 1, keepdims=False)
        fetched.append(spread(own_piece, "seq", owners[global_slot]))
    global_kv = jnp.stack(fetched)
    global_kv = global_kv.reshape(2, 2, BLOCK, head_count, HEAD_DIM).transpose(3, 0, 1, 2, 4)
    global_kv = jnp.broadcast_to(
        global_kv[:, None], (head_count, blocks_here, 2, 2, BLOCK, HEAD_DIM)
    )
    head_ids = jnp.arange(head_count, dtype=jnp.int32)
    peer_flat = rand_peer[0].reshape(pick_total)
    ident_flat = (head_ids[None, :, None] * blocks_here + rand_local[0]).reshape(pick_total)
    slot_of_pick = slot_numbers(peer_flat, slot_depth)
    targets = jnp.arange(slot_total, dtype=jnp.int32)
    slot_hits = slot_of_pick[None, :] == targets[:, None]
    ask_table = jnp.sum(jnp.where(slot_hits, ident_flat[None, :] + 1, 0), axis=1) - 1
    wanted = lax.all_to_all(
        ask_table.reshape(seq_count, slot_depth), "seq", split_axis=0, concat_axis=0, tiled=True
    )
    live_slots = (wanted >= 0).reshape(slot_total)
    safe_ids = jnp.maximum(wanted, 0).reshape(slot_total)
    by_ident = key_value.reshape(2, blocks_here, BLOCK, head_count, HEAD_DIM).transpose(
        3, 1, 0, 2, 4
    )
    by_ident = by_ident.reshape(head_count * blocks_here, 2, BLOCK, HEAD_DIM)
    served = jnp.where(
        live_slots[:, None, None, None], by_ident[safe_ids], jnp.zeros((), jnp.bfloat16)
    )
    received = lax.all_to_all(
        served.reshape(seq_count, slot_depth, 2, BLOCK, HEAD_DIM),
        "seq",
        split_axis=0,
        concat_axis=0,
        tiled=True,
    )
    randoms = received.reshape(slot_total, 2, BLOCK, HEAD_DIM)[slot_of_pick]
    randoms = randoms.reshape(blocks_here, head_count, 3, 2, BLOCK, HEAD_DIM).transpose(
        1, 0, 2, 3, 4, 5
    )
    gathered = jnp.concatenate([windows, randoms, global_kv], axis=2)
    keys_all = gathered[:, :, :, 0].reshape(head_count, blocks_here, 8 * BLOCK, HEAD_DIM)
    values_all = gathered[:, :, :, 1].reshape(head_count, blocks_here, 8 * BLOCK, HEAD_DIM)
    block_ids = seq_index * blocks_here + jnp.arange(blocks_here, dtype=jnp.int32)
    always = jnp.ones((blocks_here,), bool)
    valid_blocks = jnp.stack(
        [block_ids > 0, always, block_ids < all_blocks - 1, always, always, always, always, always],
        axis=1,
    )
    key_mask = jnp.repeat(valid_blocks, BLOCK, axis=1)
    query_heads = block_heads(query_vectors, head_count)
    grad_heads = block_heads(cotangent, head_count)

    def attend(operands):
        block_query_rows, block_key_rows, block_value_rows, block_gradient = operands
        logits = (
            jnp.einsum(
                "jxz,jnz->jxn", block_query_rows, block_key_rows, preferred_element_type=jnp.float32
            )
            * score_scale
        )
        logits = jnp.where(key_mask[:, None, :], logits, -jnp.inf)
        row_top = jnp.max(logits, axis=-1, keepdims=True)
        log_total = row_top + jnp.log(jnp.sum(jnp.exp(logits - row_top), axis=-1, keepdims=True))
        weights = jnp.exp(logits - log_total)
        weights_reduced_precision = weights.astype(jnp.bfloat16)
        attended = jnp.einsum(
            "zta,zan->ztn",
            weights_reduced_precision,
            block_value_rows,
            preferred_element_type=jnp.float32,
        )
        grad_weights = jnp.einsum(
            "jxz,jnz->jxn", block_gradient, block_value_rows, preferred_element_type=jnp.float32
        )
        centre = jnp.sum(weights * grad_weights, axis=-1, keepdims=True)
        logit_gradient = (weights * (grad_weights - centre) * score_scale).astype(jnp.bfloat16)
        grad_query = jnp.einsum(
            "zta,zan->ztn", logit_gradient, block_key_rows, preferred_element_type=jnp.float32
        )
        return (
            attended.astype(jnp.bfloat16),
            grad_query.astype(jnp.bfloat16),
            weights_reduced_precision,
            logit_gradient,
        )

    attended, grad_query, weights_reduced_precision, logit_gradient = lax.map(
        attend, (query_heads, keys_all, values_all, grad_heads)
    )
    split_weights = weights_reduced_precision.reshape(head_count, blocks_here, BLOCK, 8, BLOCK)
    split_grads = logit_gradient.reshape(head_count, blocks_here, BLOCK, 8, BLOCK)

    def key_terms(part_grads, part_weights):
        key_part = jnp.einsum(
            "hbqjk,hbqd->hbjkd", part_grads, query_heads, preferred_element_type=jnp.float32
        )
        value_part = jnp.einsum(
            "hbqjk,hbqd->hbjkd", part_weights, grad_heads, preferred_element_type=jnp.float32
        )
        return jnp.stack([key_part, value_part])

    window_terms = key_terms(split_grads[:, :, :, 0:3], split_weights[:, :, :, 0:3])
    global_terms = jnp.sum(
        key_terms(split_grads[:, :, :, 6:8], split_weights[:, :, :, 6:8]), axis=2
    )
    placed = jnp.pad(window_terms[:, :, :, 0], ((0, 0), (0, 0), (0, 2), (0, 0), (0, 0)))
    placed = placed + jnp.pad(window_terms[:, :, :, 1], ((0, 0), (0, 0), (1, 1), (0, 0), (0, 0)))
    placed = placed + jnp.pad(window_terms[:, :, :, 2], ((0, 0), (0, 0), (2, 0), (0, 0), (0, 0)))
    own_terms = placed[:, :, 1 : blocks_here + 1]
    from_next = shifted(placed[:, :, 0].astype(jnp.bfloat16), "seq", -1).astype(jnp.float32)
    from_prev = shifted(placed[:, :, blocks_here + 1].astype(jnp.bfloat16), "seq", 1).astype(
        jnp.float32
    )
    own_terms = own_terms.at[:, :, blocks_here - 1].add(from_next)
    own_terms = own_terms.at[:, :, 0].add(from_prev)
    random_terms = key_terms(split_grads[:, :, :, 3:6], split_weights[:, :, :, 3:6])
    by_pick = (
        random_terms.transpose(2, 1, 3, 0, 4, 5)
        .reshape(pick_total, 2, BLOCK, HEAD_DIM)
        .astype(jnp.bfloat16)
    )
    outgoing = (
        jnp.zeros((slot_total, 2, BLOCK, HEAD_DIM), jnp.bfloat16).at[slot_of_pick].set(by_pick)
    )
    returned = lax.all_to_all(
        outgoing.reshape(seq_count, slot_depth, 2, BLOCK, HEAD_DIM),
        "seq",
        split_axis=0,
        concat_axis=0,
        tiled=True,
    )
    arriving = returned.reshape(slot_total, 2, BLOCK, HEAD_DIM).astype(jnp.float32)
    arriving = jnp.where(live_slots[:, None, None, None], arriving, 0.0)
    by_owner = (
        jnp.zeros((head_count * blocks_here, 2, BLOCK, HEAD_DIM), jnp.float32)
        .at[safe_ids]
        .add(arriving)
    )
    own_terms = own_terms + by_owner.reshape(head_count, blocks_here, 2, BLOCK, HEAD_DIM).transpose(
        2, 0, 1, 3, 4
    )
    global_total = lax.psum(global_terms, "seq")
    positions = jnp.arange(blocks_here, dtype=jnp.int32)
    for global_slot in range(2):
        owner_hit = jnp.logical_and(
            owners[global_slot] == seq_index, positions == spot_ids[global_slot]
        )
        own_terms = own_terms + jnp.where(
            owner_hit[None, None, :, None, None], global_total[:, :, global_slot][:, :, None], 0.0
        )
    attended_rows = token_rows(attended)
    grad_query_rows = token_rows(grad_query)
    grad_key_rows = token_rows(own_terms[0]).astype(jnp.bfloat16)
    grad_value_rows = token_rows(own_terms[1]).astype(jnp.bfloat16)
    return (
        lax.all_to_all(attended_rows, "head", split_axis=0, concat_axis=1, tiled=True),
        lax.all_to_all(grad_query_rows, "head", split_axis=0, concat_axis=1, tiled=True),
        lax.all_to_all(grad_key_rows, "head", split_axis=0, concat_axis=1, tiled=True),
        lax.all_to_all(grad_value_rows, "head", split_axis=0, concat_axis=1, tiled=True),
    )


def solution(mesh):
    placed = (
        P("seq", "head"),
        P("seq", "head"),
        P("seq", "head"),
        P("seq", "head"),
        P("head", "seq", None, None),
        P("head", "seq", None, None),
        P(),
    )
    return jax.shard_map(
        on_device,
        mesh=mesh,
        in_specs=placed,
        out_specs=(
            P(("seq", "head"), None),
            P(("seq", "head"), None),
            P(("seq", "head"), None),
            P(("seq", "head"), None),
        ),
        check_vma=False,
    )
```

profile of v0, /device:TPU:1, one launch (start us, length us, event | category | flops | bytes accessed | tf_op | source)
XLA Modules:
  0.0 762.5 jit_solution(6218270166916235940)
XLA Ops:
  10.1 16.3 %all-to-all-start = ((s32[128,1,2]{2,1,0:T(1,128)}), s32[128,1,2]{2,1,0:T(1,128)S(1)}, u32[]{:S(2)}, u32[]{:S(2)}) async-start(s32[128,1,2]{2,1,0:T(1,128)} %bitcast.7), calls=%async_computation | async-start | bytes 131072 | tf_op jit(solution)/shard_map/all_to_all | solution.py:100
  28.7 8.5 %all-to-all-done = s32[128,1,2]{2,1,0:T(1,128)S(1)} async-done(((s32[128,1,2]{2,1,0:T(1,128)}), s32[128,1,2]{2,1,0:T(1,128)S(1)}, u32[]{:S(2)}, u32[]{:S(2)}) %all-to-all-start) | async-done | bytes 1056 | tf_op jit(solution)/shard_map/all_to_all | solution.py:100
  38.0 8.6 %gather_fusion = bf16[256,2,64,128]{3,2,1,0:T(8,128)(2,1)} fusion(bf16[16,2,64,128]{3,2,1,0:T(8,128)(2,1)S(1)} %bitcast.257, s32[1024]{0:T(1024)S(1)} %pad_clamp_fusion.1), kind=kCustom, calls=%fused_computation | custom fusion | bytes 16778240 | tf_op jit(solution)/shard_map/gather | solution.py:110
  46.6 7.3 broadcast_select_fusion
  53.9 7.6 all-to-all-start.1
  61.6 2.4 collective-permute-start
  64.1 1.5 collective-permute-start.1
  75.5 10.7 %collective-permute-done = bf16[2,64,1024]{2,1,0:T(8,128)(2,1)S(1)} collective-permute-done((bf16[2,64,1024]{2,1,0:T(8,128)(2,1)S(1)}, bf16[2,64,1024]{2,1,0:T(8,128)(2,1)S(1)}, u32[]{:S(2)}, u32[]{:S(2)}) %collective-permute-start) | collective-permute-done | bytes 262176 | tf_op jit(solution)/shard_map/ppermute | solution.py:18
  86.2 2.7 collective-permute-done.1
  89.8 226.5 %all-reduce.9.cloned.1.call-done = (bf16[1,2,64,8,128]{4,3,2,1,0:T(8,128)(2,1)}, bf16[1,2,64,8,128]{4,3,2,1,0:T(8,128)(2,1)}) async-done(((bf16[1,2,64,8,128]{4,3,2,1,0:T(8,128)(2,1)}, bf16[1,2,64,8,128]{4,3,2,1,0:T(8,128)(2,1)}), (bf16[1,2,64,8,128]{4,3,2,1,0:T(8,128)(2,1)}, bf16[1,2,64,8,128]{4,3,2,1,0:T(8,128)(2,1)})) %all-reduce.9.cloned.1.call-update) | async-done | bytes 524304 | tf_op jit(solution)/shard_map/psum | solution.py:29
  316.3 1.9 maximum_bitcast_fusion.3
  318.2 4.2 gather_fusion.1
  322.4 1.2 copy.256
  325.3 1.9 copy.173
  327.2 59.7 %while.19 = (s32[]{:T(128)}, bf16[8,2,64,128]{3,2,1,0:T(8,128)(2,1)}, bf16[8,2,64,128]{3,2,1,0:T(8,128)(2,1)}, bf16[8,2,64,512]{3,2,1,0:T(8,128)(2,1)}, bf16[8,2...) while((s32[]{:T(128)}, ...), condition=%wide.region_8.9_spmd.clone, body=%wide.region_4.8_spmd.clone.sunk | while | flops 68650112 | bytes 4866701 | solution.py:170
  327.4 1.3 fusion.95
  329.8 2.0 fusion.98
  332.7 1.2 bitcast_dynamic-update-slice_fusion.5
  334.9 1.3 fusion.95
  337.3 2.0 fusion.98
  340.2 1.2 bitcast_dynamic-update-slice_fusion.5
  342.3 1.3 fusion.95
  344.8 2.0 fusion.98
  347.6 1.2 bitcast_dynamic-update-slice_fusion.5
  349.8 1.3 fusion.95
  352.2 2.0 fusion.98
  355.1 1.2 bitcast_dynamic-update-slice_fusion.5
  357.2 1.3 fusion.95
  359.7 2.0 fusion.98
  362.5 1.2 bitcast_dynamic-update-slice_fusion.5
  364.7 1.3 fusion.95
  367.1 2.0 fusion.98
  370.0 1.2 bitcast_dynamic-update-slice_fusion.5
  372.1 1.3 fusion.95
  374.6 2.0 fusion.98
  377.5 1.2 bitcast_dynamic-update-slice_fusion.5
  379.6 1.3 fusion.95
  382.0 2.0 fusion.98
  384.9 1.2 bitcast_dynamic-update-slice_fusion.5
  386.9 1.8 copy_bitcast_fusion.4
  388.7 9.2 %all-to-all-start.2 = ((bf16[2,64,1024]{2,1,0:T(8,128)(2,1)}), bf16[2,64,1024]{2,1,0:T(8,128)(2,1)}, u32[]{:S(2)}, u32[]{:S(2)}) async-start(bf16[2,64,1024]{2,1,0:T(8,128)(2,1)} %copy_bitcast_fusion.4), calls=%async_computation.2 | async-start | bytes 524288 | tf_op jit(solution)/shard_map/all_to_all | solution.py:239
  397.9 1.7 copy_bitcast_fusion.3
  399.6 1.1 copy.181
  400.7 2.8 copy.183
  403.8 1.2 copy-done
  405.6 1.3 copy.192
  406.9 5.4 broadcast_in_dim.142
  412.3 7.6 scatter_fusion
  419.9 3.6 all_to_all.86
  423.5 10.5 %all-to-all-start.4 = ((bf16[128,2,2,64,128]{4,3,2,1,0:T(8,128)(2,1)}), bf16[128,2,2,64,128]{4,3,2,1,0:T(8,128)(2,1)}, u32[]{:S(2)}, u32[]{:S(2)}) async-start(bf16[128,2,2,64,128]{4,3,2,1,0:T(8,128)(2,1)} %bitcast.258), calls=%async_computation.4 | async-start | bytes 16777216 | tf_op jit(solution)/shard_map/all_to_all | solution.py:208
  434.5 1.3 convolution_bitcast_fusion.2
  435.8 1.2 maximum_reduce_fusion
  437.4 1.2 copy-done.1
  439.8 1.3 collective-permute-start.2
  442.9 4.0 collective-permute-start.3
  447.7 1.7 copy.224
  450.2 14.7 %collective-permute-done.2 = bf16[2,8,64,128]{3,2,1,0:T(8,128)(2,1)S(1)} collective-permute-done((bf16[2,8,64,128]{3,2,1,0:T(8,128)(2,1)S(1)}, bf16[2,8,64,128]{3,2,1,0:T(8,128)(2,1)S(1)}, u32[]{:S(2)}, u32[]{:S(2)}) %collective-permute-start.2) | collective-permute-done | bytes 262176 | tf_op jit(solution)/shard_map/ppermute | solution.py:35
  465.0 1.1 fusion.49
  466.2 229.8 %all-reduce.7.cloned.1.call-done = f32[2,8,2,64,128]{4,3,2,1,0:T(8,128)} async-done(((f32[2,8,2,64,128]{4,3,2,1,0:T(8,128)}), f32[2,8,2,64,128]{4,3,2,1,0:T(8,128)}) %all-reduce.7.cloned.1.call-update) | async-done | bytes 1048592 | tf_op jit(solution)/shard_map/psum | solution.py:225
  696.0 1.3 slice_bitcast_fusion.1
  697.3 10.3 %convert_select_fusion = f32[256,2,64,128]{3,2,1,0:T(8,128)} fusion(bf16[128,2,2,64,128]{4,3,2,1,0:T(8,128)(2,1)} %all-to-all-done.4, pred[256]{0:T(512)(128)(4,1)S(1)} %ge.16), kind=kLoop, calls=%fused_computation.46 | loop fusion | flops 8388608 | bytes 25166080 | tf_op jit(solution)/shard_map/jit(_where)/select_n | solution.py:216
  707.7 33.2 %scatter_fusion.1 = f32[16,2,64,128]{3,2,1,0:T(8,128)S(1)} fusion(f32[16,2,64,128]{3,2,1,0:T(8,128)S(1)} %broadcast_in_dim.140, s32[256]{0:T(256)S(1)} %reshape.330, f32[256,2,64,128]{3,2,1,0:T(8,128)} %convert_select_fusion), kind=kCustom, calls=%fused_computation.3 | custom fusion | flops 4194304 | bytes 50332672 | tf_op jit(solution)/shard_map/scatter-add | solution.py:220
  741.4 8.8 %all_to_all.87 = bf16[2,64,1024]{2,1,0:T(8,128)(2,1)S(1)} all-to-all(bf16[2,64,1024]{2,1,0:T(8,128)(2,1)S(1)} %bitcast.286), channel_id=1, replica_groups=mesh['seq'=128,'head'=2] {'head'}, dimensions={0} | all-to-all | bytes 524288 | tf_op jit(solution)/shard_map/all_to_all | solution.py:242
  751.0 3.9 all_to_all.88
  (166 shorter events, 44.4 us)
Async XLA Ops:
  10.1 27.0 %all-to-all-start = ((s32[128,1,2]{2,1,0:T(1,128)}), s32[128,1,2]{2,1,0:T(1,128)S(1)}, u32[]{:S(2)}, u32[]{:S(2)}) async-start(s32[128,1,2]{2,1,0:T(1,128)} %bitcast.7), calls=%async_computation | async-start | bytes 131072 | tf_op jit(solution)/shard_map/all_to_all | solution.py:100
  53.9 7.7 %copy-start.3 = (bf16[128,1024]{1,0:T(8,128)(2,1)S(1)}, bf16[128,1024]{1,0:T(8,128)(2,1)}, u32[]{:S(2)}) copy-start(bf16[128,1024]{1,0:T(8,128)(2,1)} %param.14) | copy-start | bytes 786436
  53.9 7.7 %copy-start.4 = (bf16[128,1024]{1,0:T(8,128)(2,1)S(1)}, bf16[128,1024]{1,0:T(8,128)(2,1)}, u32[]{:S(2)}) copy-start(bf16[128,1024]{1,0:T(8,128)(2,1)} %param.15) | copy-start | bytes 786436
  53.9 11.7 %copy-start.12 = (s32[2]{0:T(128)S(1)}, s32[2]{0:T(128)}, u32[]{:S(2)}) copy-start(s32[2]{0:T(128)} %param.19) | copy-start | bytes 28
  53.9 264.3 %all-to-all-start.1 = ((bf16[128,2,2,64,128]{4,3,2,1,0:T(8,128)(2,1)}), bf16[128,2,2,64,128]{4,3,2,1,0:T(8,128)(2,1)}, u32[]{:S(2)}, u32[]{:S(2)}) async-start(bf16[128,2,2,64,128]{4,3,2,1,0:T(8,128)(2,1)} %broadcast_select_fusion), calls=%async_computation.1 | async-start | bytes 16777216 | tf_op jit(solution)/shard_map/all_to_all | solution.py:112
  61.5 11.2 %copy-start.11 = (s32[1,2,8,3]{2,1,3,0:T(2,128)S(1)}, s32[1,2,8,3]{2,1,3,0:T(2,128)}, u32[]{:S(2)}) copy-start(s32[1,2,8,3]{2,1,3,0:T(2,128)} %param.17) | copy-start | bytes 580
  61.5 11.4 %copy-start.9 = (bf16[128,1024]{1,0:T(8,128)(2,1)S(1)}, bf16[128,1024]{1,0:T(8,128)(2,1)}, u32[]{:S(2)}) copy-start(bf16[128,1024]{1,0:T(8,128)(2,1)} %param.13) | copy-start | bytes 786436
  61.5 254.8 %all-reduce.9.cloned.1.call-start = ((), (), s32[]{:S(2)}) async-start(), calls=%async_computation.8 | async-start | bytes 1048576 | tf_op jit(solution)/shard_map/psum | solution.py:29
  61.6 11.4 %copy-start.10 = (bf16[128,1024]{1,0:T(8,128)(2,1)S(1)}, bf16[128,1024]{1,0:T(8,128)(2,1)}, u32[]{:S(2)}) copy-start(bf16[128,1024]{1,0:T(8,128)(2,1)} %param.16) | copy-start | bytes 786436
  61.6 24.6 %collective-permute-start = (bf16[2,64,1024]{2,1,0:T(8,128)(2,1)S(1)}, bf16[2,64,1024]{2,1,0:T(8,128)(2,1)S(1)}, u32[]{:S(2)}, u32[]{:S(2)}) collective-permute-start(bf16[2,64,1024]{2,1,0:T(8,128)(2,1)S(1)} %get-tuple-element.200), channel_id=1, source_target_pairs={{0,2},{2,4},{4,6},{6,8},{8,10},{10,12},{12,14},{14,16},{16,18},{18... | collective-permute-start | bytes 786440 | tf_op jit(solution)/shard_map/ppermute | solution.py:18
  64.1 24.9 %collective-permute-start.1 = (bf16[2,64,1024]{2,1,0:T(8,128)(2,1)S(1)}, bf16[2,64,1024]{2,1,0:T(8,128)(2,1)S(1)}, u32[]{:S(2)}, u32[]{:S(2)}) collective-permute-start(bf16[2,64,1024]{2,1,0:T(8,128)(2,1)S(1)} %get-tuple-element.201), channel_id=1, source_target_pairs={{2,0},{4,2},{6,4},{8,6},{10,8},{12,10},{14,12},{16,14},{18,16},{20... | collective-permute-start | bytes 786440 | tf_op jit(solution)/shard_map/ppermute | solution.py:20
  322.4 1.3 copy-start.6
  386.9 12.7 %copy-start.7 = (bf16[8,2,64,512]{3,2,1,0:T(8,128)(2,1)S(1)}, bf16[8,2,64,512]{3,2,1,0:T(8,128)(2,1)}, u32[]{:S(2)}) copy-start(bf16[8,2,64,512]{3,2,1,0:T(8,128)(2,1)} %get-tuple-element.85) | copy-start | bytes 3145732
  388.7 31.2 %all-to-all-start.2 = ((bf16[2,64,1024]{2,1,0:T(8,128)(2,1)}), bf16[2,64,1024]{2,1,0:T(8,128)(2,1)}, u32[]{:S(2)}, u32[]{:S(2)}) async-start(bf16[2,64,1024]{2,1,0:T(8,128)(2,1)} %copy_bitcast_fusion.4), calls=%async_computation.2 | async-start | bytes 524288 | tf_op jit(solution)/shard_map/all_to_all | solution.py:239
  400.7 2.8 copy-start.5
  403.5 1.6 copy-start
  412.3 7.6 %copy-start.8 = (bf16[2,64,1024]{2,1,0:T(8,128)(2,1)S(1)}, bf16[2,64,1024]{2,1,0:T(8,128)(2,1)}, u32[]{:S(2)}) copy-start(bf16[2,64,1024]{2,1,0:T(8,128)(2,1)} %copy_bitcast_fusion.3) | copy-start | bytes 786436
  423.5 273.8 %all-to-all-start.4 = ((bf16[128,2,2,64,128]{4,3,2,1,0:T(8,128)(2,1)}), bf16[128,2,2,64,128]{4,3,2,1,0:T(8,128)(2,1)}, u32[]{:S(2)}, u32[]{:S(2)}) async-start(bf16[128,2,2,64,128]{4,3,2,1,0:T(8,128)(2,1)} %bitcast.258), calls=%async_computation.4 | async-start | bytes 16777216 | tf_op jit(solution)/shard_map/all_to_all | solution.py:208
  433.9 262.1 %all-reduce.7.cloned.1.call-start = ((), (), s32[]{:S(2)}) async-start(), calls=%async_computation.7 | async-start | bytes 2097152 | tf_op jit(solution)/shard_map/psum | solution.py:225
  437.0 1.6 copy-start.1
  439.8 10.3 %copy-start.2 = (f32[2,8,4,64,128]{4,3,2,1,0:T(8,128)}, f32[2,8,4,64,128]{4,3,2,1,0:T(8,128)S(1)}, u32[]{:S(2)}) copy-start(f32[2,8,4,64,128]{4,3,2,1,0:T(8,128)S(1)} %get-tuple-element.183) | copy-start | bytes 6291460
  439.8 25.1 %collective-permute-start.2 = (bf16[2,8,64,128]{3,2,1,0:T(8,128)(2,1)S(1)}, bf16[2,8,64,128]{3,2,1,0:T(8,128)(2,1)S(1)}, u32[]{:S(2)}, u32[]{:S(2)}) collective-permute-start(bf16[2,8,64,128]{3,2,1,0:T(8,128)(2,1)S(1)} %get-tuple-element.194), channel_id=1, source_target_pairs={{2,0},{4,2},{6,4},{8,6},{10,8},{12,10},{14,12},{16,14},{18,16},{20... | collective-permute-start | bytes 786440 | tf_op jit(solution)/shard_map/ppermute | solution.py:35
  442.9 23.1 %collective-permute-start.3 = (bf16[2,8,64,128]{3,2,1,0:T(8,128)(2,1)S(1)}, bf16[2,8,64,128]{3,2,1,0:T(8,128)(2,1)S(1)}, u32[]{:S(2)}, u32[]{:S(2)}) collective-permute-start(bf16[2,8,64,128]{3,2,1,0:T(8,128)(2,1)S(1)} %get-tuple-element.193), channel_id=1, source_target_pairs={{0,2},{2,4},{4,6},{6,8},{8,10},{10,12},{12,14},{14,16},{16,18},{18... | collective-permute-start | bytes 786440 | tf_op jit(solution)/shard_map/ppermute | solution.py:35
Sparse Core Ops, SparseCore 0:
  72.8 243.4 all-reduce.8
  441.0 254.9 all-reduce.6
where the time goes:
time: 765 us; the launch traced here: 763 us
  waiting for transfers between devices  493 us (64%)
  other arithmetic  76.7 us (10%)
  local copies, waits for them, and re-layouts  58.7 us (8%)
  starting transfers between devices  53.2 us (7%)
  matrix products  43.8 us (6%)
  between operations  20.7 us (3%)
  blocking collectives  16.4 us (2%)
    psum x1, waiting for transfers between devices, on_device(): global_total = lax.psum(global_terms, 'seq')  230 us
    psum x1, waiting for transfers between devices, spread(): return lax.psum(kept, axis)  227 us
    scatter-add x1, other arithmetic, on_device(): by_owner = jnp.zeros((head_count * blocks_here, 2, BLOCK, HEAD_DIM), jnp....  33.2 us
    all_to_all x1, starting transfers between devices, on_device(): lax.all_to_all(ask_table.reshape(seq_count, slot_depth), 'seq', split_axi...  16.3 us
    dot_general x8, matrix products, attend(): jnp.einsum('zta,zan->ztn', logit_gradient, block_key_rows, preferred_elem...  16.1 us
  transfers between devices with their start and end apart: 10, of which 6 were waited for; matrix products, arithmetic and copies ran while one was open for 5% of the time, Pallas kernels for 0%

commit v1 on v0

v1 whole, which is shorter than its diff:
```python
import functools

import jax
import jax.numpy as jnp
from jax import lax
from jax.experimental import pallas as pl
from jax.experimental.pallas import tpu as pltpu
from jax.sharding import PartitionSpec as P

MESH = pl.DeviceIdType.MESH
HEAD_DIM = 128
BLOCK = 64
HEADS_HERE = 8
BLOCKS_HERE = 2
WIDTH = HEADS_HERE * HEAD_DIM
PLANE = 16
DEPTH = 8
ITEMS = BLOCKS_HERE * HEADS_HERE
PICKS = 3 * ITEMS
ROWS = 32
CHUNKS = 4
VMEM_BYTES = 56 * 1024 * 1024
F32 = jnp.float32
BF16 = jnp.bfloat16


def position():
    seq = lax.axis_index("seq")
    return seq, lax.div(seq, PLANE), lax.rem(seq, PLANE), lax.axis_index("head")


def signal(seq, head):
    pl.semaphore_signal(
        pltpu.get_barrier_semaphore(), inc=1, device_id=(seq, head), device_id_type=MESH
    )


def remote(src, dst, send, recv, seq, head):
    return pltpu.make_async_remote_copy(
        src_ref=src,
        dst_ref=dst,
        send_sem=send,
        recv_sem=recv,
        device_id=(seq, head),
        device_id_type=MESH,
    )


def swap_tables_kernel(table, got, most, send1, recv1, send2, recv2):
    seq, z, p, head = position()
    place = z * 2 + head

    def plane_copy(i):
        peer = lax.rem(p + i, PLANE)
        return remote(
            table.at[peer], got.at[p], send1.at[i], recv1.at[i], z * PLANE + peer, head
        )

    def column_copy(i):
        other = lax.rem(place + i, 2 * DEPTH)
        return remote(
            most.at[place],
            most.at[place],
            send2.at[i],
            recv2.at[i],
            lax.div(other, 2) * PLANE + p,
            lax.rem(other, 2),
        )

    @pl.loop(1, PLANE)
    def _(i):
        signal(z * PLANE + lax.rem(p + i, PLANE), head)
        other = lax.rem(place + i, 2 * DEPTH)
        signal(lax.div(other, 2) * PLANE + p, lax.rem(other, 2))

    pl.semaphore_wait(pltpu.get_barrier_semaphore(), 2 * (PLANE - 1))

    @pl.loop(1, PLANE)
    def _(i):
        plane_copy(i).start()

    got[p] = table[p]

    @pl.loop(1, PLANE)
    def _(i):
        plane_copy(i).wait()

    most[place] = jnp.max(got[...], axis=0)

    @pl.loop(1, 2 * DEPTH)
    def _(i):
        column_copy(i).start()

    @pl.loop(1, 2 * DEPTH)
    def _(i):
        column_copy(i).wait()


def swap_tables(table):
    shape = jax.ShapeDtypeStruct((PLANE, 8, 128), jnp.int32)
    vmem = pl.BlockSpec(memory_space=pltpu.VMEM)
    return pl.pallas_call(
        swap_tables_kernel,
        out_shape=(shape, shape),
        in_specs=[vmem],
        out_specs=(vmem, vmem),
        scratch_shapes=[pltpu.SemaphoreType.DMA((PLANE,))] * 4,
        compiler_params=pltpu.CompilerParams(collective_id=0, has_side_effects=True),
        name="swap_tables",
    )(table)


def greet(z, p, seq, head, partner):
    @pl.loop(1, PLANE)
    def _(i):
        signal(z * PLANE + lax.rem(p + i, PLANE), head)

    for step in (1, DEPTH - 1):
        signal(lax.rem(z + step, DEPTH) * PLANE + p, head)
    for step in (1, PLANE * DEPTH - 1):
        signal(lax.rem(seq + step, PLANE * DEPTH), head)
    if partner:
        signal(seq, 1 - head)
    pl.semaphore_wait(pltpu.get_barrier_semaphore(), PLANE + 3 + (1 if partner else 0))


def ring_hops(q, d):
    return 4 if (d == 0) == (q % 2 == 0) else 3


def ring_slot(q, d, t):
    return sum(ring_hops(q, e) for e in range(d)) + 7 * q + t


def fetch_kernel(c, slots, glob, key, value, halo, shared, *rest):
    picked, held, out = rest[0:4], rest[4:8], rest[8:12]
    relay, zsend, zrecv, psend, precv, gsend, grecv, hsend, hrecv = rest[12:]
    seq, z, p, head = position()
    greet(z, p, seq, head, False)

    def halo_copy(side, kv):
        block = (1 - side) * BLOCK
        other = lax.rem(seq + (1 if side == 0 else PLANE * DEPTH - 1), PLANE * DEPTH)
        return remote(
            (key, value)[kv].at[pl.ds(block, BLOCK)],
            halo.at[side * 2 + kv],
            hsend.at[side * 2 + kv],
            hrecv.at[side * 2 + kv],
            other,
            head,
        )

    def ring_copy(q, d, t):
        step = 1 if d == 0 else DEPTH - 1
        owner = lax.rem(z + t * (DEPTH - step), DEPTH)
        rows = pl.ds(owner * ITEMS, ITEMS)
        slot = ring_slot(q, d, t)
        return remote(
            held[q].at[rows],
            held[q].at[rows],
            zsend.at[slot],
            zrecv.at[slot],
            lax.rem(z + step, DEPTH) * PLANE + p,
            head,
        )

    def plane_copy(q, i):
        peer = lax.rem(p + i, PLANE)
        return remote(
            out[q].at[pl.ds(peer * (c + 1), c + 1)],
            picked[q].at[pl.ds(p * (c + 1), c + 1)],
            psend.at[q * PLANE + i],
            precv.at[q * PLANE + i],
            z * PLANE + peer,
            head,
        )

    def shared_copy(q, i):
        peer = lax.rem(p + i, PLANE)
        return remote(
            relay.at[q],
            shared.at[q * PLANE + p],
            gsend.at[q * PLANE + i],
            grecv.at[q * PLANE + i],
            z * PLANE + peer,
            head,
        )

    def fill(q):
        source, half = (key, value)[q // 2], q % 2
        for b in range(BLOCKS_HERE):
            for j in range(HEADS_HERE):
                held[q][z * ITEMS + b * HEADS_HERE + j] = source[
                    b * BLOCK + half * ROWS : b * BLOCK + (half + 1) * ROWS,
                    j * HEAD_DIM : (j + 1) * HEAD_DIM,
                ]

    def ring_start(q):
        for d in range(2):
            ring_copy(q, d, 0).start()

    def ring(chunks):
        for t in range(4):
            for q in chunks:
                for d in range(2):
                    if t < ring_hops(q, d):
                        ring_copy(q, d, t).wait_recv()
                        if t + 1 < ring_hops(q, d):
                            ring_copy(q, d, t + 1).start()

    def spread(q):
        @pl.loop(1, PLANE)
        def _(i):
            peer = lax.rem(p + i, PLANE)
            for s in range(c):
                out[q][peer * (c + 1) + s] = held[q][slots[peer, s]]
            out[q][peer * (c + 1) + c] = held[q][glob[peer]]
            plane_copy(q, i).start()

        for s in range(c):
            picked[q][p * (c + 1) + s] = held[q][slots[p, s]]
        picked[q][p * (c + 1) + c] = held[q][glob[p]]

    def share(q):
        @pl.loop(1, PLANE)
        def _(i):
            plane_copy(q, i).wait_recv()

        relay[q] = picked[q][glob[PLANE + p] * (c + 1) + c]
        shared[q * PLANE + p] = relay[q]

        @pl.loop(1, PLANE)
        def _(i):
            shared_copy(q, i).start()

    fill(0)
    ring_start(0)
    fill(1)
    ring_start(1)
    for side in range(2):
        for kv in range(2):
            halo_copy(side, kv).start()
    fill(2)
    fill(3)
    ring((0, 1))
    ring_start(2)
    ring_start(3)
    spread(0)
    spread(1)
    ring((2, 3))
    spread(2)
    spread(3)
    for q in range(CHUNKS):
        share(q)
    for q in range(CHUNKS):

        @pl.loop(1, PLANE)
        def _(i):
            shared_copy(q, i).wait()
            plane_copy(q, i).wait_send()

        for d in range(2):
            for t in range(ring_hops(q, d)):
                ring_copy(q, d, t).wait_send()
    for side in range(2):
        for kv in range(2):
            halo_copy(side, kv).wait()


def fetch(c, slots, glob, key, value, collective_id):
    smem = pl.BlockSpec(memory_space=pltpu.SMEM)
    vmem = pl.BlockSpec(memory_space=pltpu.VMEM)
    part = jax.ShapeDtypeStruct((PLANE * (c + 1), ROWS, HEAD_DIM), BF16)
    dma = pltpu.SemaphoreType.DMA
    return pl.pallas_call(
        functools.partial(fetch_kernel, c),
        out_shape=(
            jax.ShapeDtypeStruct((4, BLOCK, WIDTH), BF16),
            jax.ShapeDtypeStruct((CHUNKS * PLANE, ROWS, HEAD_DIM), BF16),
        )
        + (part,) * CHUNKS,
        in_specs=[smem, smem, vmem, vmem],
        out_specs=(vmem,) * (2 + CHUNKS),
        scratch_shapes=[pltpu.VMEM((DEPTH * ITEMS, ROWS, HEAD_DIM), BF16)] * CHUNKS
        + [pltpu.VMEM(part.shape, BF16)] * CHUNKS
        + [
            pltpu.VMEM((CHUNKS, ROWS, HEAD_DIM), BF16),
            dma((7 * CHUNKS,)),
            dma((7 * CHUNKS,)),
            dma((CHUNKS * PLANE,)),
            dma((CHUNKS * PLANE,)),
            dma((CHUNKS * PLANE,)),
            dma((CHUNKS * PLANE,)),
            dma((4,)),
            dma((4,)),
        ],
        compiler_params=pltpu.CompilerParams(
            collective_id=collective_id, has_side_effects=True, vmem_limit_bytes=VMEM_BYTES
        ),
        name=f"fetch_{c}",
    )(slots, glob, key, value)


def dot(a, b, contract):
    return lax.dot_general(a, b, ((contract[0:1], contract[1:2]), ((), ())), preferred_element_type=F32)


def attend_kernel(
    where, query, grad, key, value, halo, shared, *rest
):
    picked = rest[0:4]
    attended, grad_query, own, sides, both = rest[4:9]
    terms = rest[9:13]
    seq = lax.axis_index("seq")
    scale = HEAD_DIM ** (-0.5)
    near = 4 * BLOCK
    rows = lax.broadcasted_iota(jnp.int32, (near, 128), 0)
    lanes = lax.broadcasted_iota(jnp.int32, (near, 128), 1)
    last = PLANE * DEPTH - 1
    first_block, second_block = lanes < BLOCK, lanes >= BLOCK
    hidden = (
        (first_block & (rows >= 3 * BLOCK))
        | (second_block & (rows < BLOCK))
        | ((rows < BLOCK) & (seq == 0))
        | ((rows >= 3 * BLOCK) & (seq == last))
    )
    pick_lanes = lax.broadcasted_iota(jnp.int32, (3 * BLOCK, 128), 1) < BLOCK

    @pl.loop(0, HEADS_HERE)
    def _(j):
        cols = pl.ds(pl.multiple_of(j * HEAD_DIM, HEAD_DIM), HEAD_DIM)
        q = query[:, cols]
        g = grad[:, cols]

        def listed(kv):
            near_part = [
                halo[kv, :, cols],
                (key, value)[kv][:, cols],
                halo[2 + kv, :, cols],
            ]
            for group in range(2):
                for half in range(2):
                    near_part.append(
                        shared[(kv * 2 + half) * PLANE + group * HEADS_HERE + j]
                    )
            far = []
            for b in range(BLOCKS_HERE):
                parts = []
                for t in range(3):
                    at = where[b * 24 + j * 3 + t]
                    for half in range(2):
                        parts.append(picked[kv * 2 + half][at])
                far.append(jnp.concatenate(parts, axis=0))
            return jnp.concatenate(near_part, axis=0), far

        keys, far_keys = listed(0)
        values, far_values = listed(1)

        def products(near_rows, far_rows, other):
            a = dot(near_rows, other, (1, 1))
            b = jnp.where(
                pick_lanes, dot(far_rows[0], other, (1, 1)), dot(far_rows[1], other, (1, 1))
            )
            return a, b

        s_near, s_far = products(keys, far_keys, q)
        s_near = s_near * scale
        s_far = s_far * scale
        s_near = jnp.concatenate(
            [jnp.where(hidden, -1e30, s_near[:near]), s_near[near:]], axis=0
        )
        top = jnp.maximum(
            jnp.max(s_near, axis=0, keepdims=True), jnp.max(s_far, axis=0, keepdims=True)
        )
        w_near = jnp.exp(s_near - top)
        w_far = jnp.exp(s_far - top)
        total = jnp.sum(w_near, axis=0, keepdims=True) + jnp.sum(w_far, axis=0, keepdims=True)
        inverse = 1.0 / total
        w_near = w_near * inverse
        w_far = w_far * inverse
        gw_near, gw_far = products(values, far_values, g)
        centre = jnp.sum(w_near * gw_near, axis=0, keepdims=True) + jnp.sum(
            w_far * gw_far, axis=0, keepdims=True
        )
        d_near = (w_near * (gw_near - centre) * scale).astype(BF16)
        d_far = (w_far * (gw_far - centre) * scale).astype(BF16)
        w_near = w_near.astype(BF16)
        w_far = w_far.astype(BF16)

        def gather(near_w, far_w, near_rows, far_rows):
            total_rows = dot(near_w, near_rows, (0, 0))
            top_rows = dot(far_w, far_rows[0], (0, 0))
            low_rows = dot(far_w, far_rows[1], (0, 0))
            return total_rows + jnp.concatenate([top_rows[:BLOCK], low_rows[BLOCK:]], axis=0)

        attended[:, cols] = gather(w_near, w_far, values, far_values).astype(BF16)
        grad_query[:, cols] = gather(d_near, d_far, keys, far_keys).astype(BF16)

        for kv in range(2):
            weight_near, weight_far = ((d_near, d_far), (w_near, w_far))[kv]
            rows_here = (q, g)[kv]
            near_terms = dot(weight_near, rows_here, (1, 0))
            zero = jnp.zeros_like(weight_far)
            for half in range(2):
                chunk = kv * 2 + half

                def piece(block):
                    return near_terms[block * BLOCK + half * ROWS : block * BLOCK + (half + 1) * ROWS]

                sides[chunk * HEADS_HERE + j] = piece(0).astype(BF16)
                sides[(CHUNKS + chunk) * HEADS_HERE + j] = piece(3).astype(BF16)
                for b in range(BLOCKS_HERE):
                    own[chunk * ITEMS + b * HEADS_HERE + j] = piece(1 + b)
                for group in range(2):
                    both[chunk * PLANE + group * HEADS_HERE + j] = piece(4 + group).astype(BF16)
            for b in range(BLOCKS_HERE):
                mine = jnp.where(pick_lanes, weight_far, zero) if b == 0 else jnp.where(
                    pick_lanes, zero, weight_far
                )
                far_terms = dot(mine, rows_here, (1, 0)).astype(BF16)
                for t in range(3):
                    for half in range(2):
                        start = t * BLOCK + half * ROWS
                        terms[kv * 2 + half][b * 24 + j * 3 + t] = far_terms[start : start + ROWS]


def attend(where, query, grad, key, value, halo, shared, picked):
    smem = pl.BlockSpec(memory_space=pltpu.SMEM)
    vmem = pl.BlockSpec(memory_space=pltpu.VMEM)
    rows = jax.ShapeDtypeStruct(query.shape, BF16)
    return pl.pallas_call(
        attend_kernel,
        out_shape=(
            rows,
            rows,
            jax.ShapeDtypeStruct((CHUNKS * ITEMS, ROWS, HEAD_DIM), F32),
            jax.ShapeDtypeStruct((2 * CHUNKS * HEADS_HERE, ROWS, HEAD_DIM), BF16),
            jax.ShapeDtypeStruct((CHUNKS * PLANE, ROWS, HEAD_DIM), BF16),
        )
        + (jax.ShapeDtypeStruct((PICKS, ROWS, HEAD_DIM), BF16),) * CHUNKS,
        in_specs=[smem] + [vmem] * (6 + CHUNKS),
        out_specs=(vmem,) * (5 + CHUNKS),
        compiler_params=pltpu.CompilerParams(vmem_limit_bytes=VMEM_BYTES),
        name="attend",
    )(where, query, grad, key, value, halo, shared, *picked)


def give_back_kernel(c, picks, order, first, ends, shared_ends, attended, grad_query, own, sides, both, *rest):
    terms, outs = rest[0:4], rest[4:8]
    out, arrived, totals, gathered = rest[8:12], rest[12:16], rest[16:20], rest[20:24]
    (
        relay, runs, zout, zin, beside, cross,
        zsend, zrecv, psend, precv, gsend, grecv, hsend, hrecv, csend, crecv,
    ) = rest[24:]
    seq, z, p, head = position()
    greet(z, p, seq, head, True)
    count = PLANE * c
    mine = pl.ds(pl.multiple_of(head * WIDTH, WIDTH), WIDTH)

    def result_copy(k):
        source = (attended, grad_query)[k].at[pl.ds((1 - head) * BLOCK, BLOCK)]
        return remote(source, outs[k].at[:, mine], csend.at[k], crecv.at[k], seq, 1 - head)

    def cross_copy(q):
        return remote(
            cross.at[q],
            outs[2 + q // 2].at[pl.ds((q % 2) * ROWS, ROWS), mine],
            csend.at[2 + q],
            crecv.at[2 + q],
            seq,
            1 - head,
        )

    def side_copy(side):
        size = CHUNKS * HEADS_HERE
        other = lax.rem(seq + (PLANE * DEPTH - 1 if side == 0 else 1), PLANE * DEPTH)
        return remote(
            sides.at[pl.ds(side * size, size)],
            beside.at[pl.ds((1 - side) * size, size)],
            hsend.at[side],
            hrecv.at[side],
            other,
            head,
        )

    def plane_copy(q, i):
        peer = lax.rem(p + i, PLANE)
        return remote(
            out[q].at[pl.ds(peer * (c + 1), c + 1)],
            arrived[q].at[pl.ds(p * (c + 1), c + 1)],
            psend.at[q * PLANE + i],
            precv.at[q * PLANE + i],
            z * PLANE + peer,
            head,
        )

    def shared_copy(q, i):
        peer = lax.rem(p + i, PLANE)
        return remote(
            relay.at[q],
            gathered[q].at[p],
            gsend.at[q * PLANE + i],
            grecv.at[q * PLANE + i],
            z * PLANE + peer,
            head,
        )

    def ring_copy(q, d, t):
        step = 1 if d == 0 else DEPTH - 1
        slot = ring_slot(q, d, t)
        return remote(
            zout.at[slot],
            zin.at[slot],
            zsend.at[slot],
            zrecv.at[slot],
            lax.rem(z + step, DEPTH) * PLANE + p,
            head,
        )

    def spread(q):
        @pl.loop(1, PLANE)
        def _(i):
            peer = lax.rem(p + i, PLANE)
            for s in range(c):
                out[q][peer * (c + 1) + s] = terms[q][picks[peer, s]]
            out[q][peer * (c + 1) + c] = both[q * PLANE + peer]
            plane_copy(q, i).start()

        for s in range(c):
            arrived[q][p * (c + 1) + s] = terms[q][picks[p, s]]
        arrived[q][p * (c + 1) + c] = both[q * PLANE + p]

    def share(q):
        @pl.loop(1, PLANE)
        def _(i):
            plane_copy(q, i).wait_recv()

        def add(i, total):
            return total + arrived[q][i * (c + 1) + c].astype(F32)

        total = lax.fori_loop(0, PLANE, add, jnp.zeros((ROWS, HEAD_DIM), F32))
        relay[q] = total.astype(BF16)
        gathered[q][p] = relay[q]
        gathered[q][PLANE] = jnp.zeros((ROWS, HEAD_DIM), BF16)

        @pl.loop(1, PLANE)
        def _(i):
            shared_copy(q, i).start()

    def collect(q):
        def add(r, total):
            term = arrived[q][order[r]].astype(F32)
            total = jnp.where(first[r] == 1, term, total + term)
            runs[r] = total
            return total

        lax.fori_loop(0, count, add, jnp.zeros((ROWS, HEAD_DIM), F32), unroll=4)

        @pl.loop(1, PLANE)
        def _(i):
            shared_copy(q, i).wait_recv()

        @pl.loop(0, DEPTH * ITEMS, unroll=4)
        def _(i):
            totals[q][i] = runs[ends[i]] + gathered[q][shared_ends[i]].astype(F32)

    def ring(chunks):
        for t in range(4):
            for q in chunks:
                for d in range(2):
                    hops = ring_hops(q, d)
                    if t < hops:
                        away = hops - t
                        target = lax.rem(z + (away if d == 0 else DEPTH - away), DEPTH)
                        rows = pl.ds(target * ITEMS, ITEMS)
                        partial = totals[q][rows]
                        if t > 0:
                            ring_copy(q, d, t - 1).wait_recv()
                            partial = partial + zin[ring_slot(q, d, t - 1)].astype(F32)
                        zout[ring_slot(q, d, t)] = partial.astype(BF16)
                        ring_copy(q, d, t).start()

    def finish(q):
        for d in range(2):
            ring_copy(q, d, ring_hops(q, d) - 1).wait_recv()
        kv, half = q // 2, q % 2
        for j in range(HEADS_HERE):
            for mine_too in range(2):
                b = head if mine_too else 1 - head
                item = b * HEADS_HERE + j
                total = totals[q][z * ITEMS + item] + own[q * ITEMS + item]
                total = total + beside[(b * CHUNKS + q) * HEADS_HERE + j].astype(F32)
                for d in range(2):
                    total = total + zin[ring_slot(q, d, ring_hops(q, d) - 1), item].astype(F32)
                total = total.astype(BF16)
                if mine_too:
                    cols = pl.ds(pl.multiple_of(head * WIDTH + j * HEAD_DIM, HEAD_DIM), HEAD_DIM)
                    outs[2 + kv][half * ROWS : (half + 1) * ROWS, cols] = total
                else:
                    cross[q, :, j * HEAD_DIM : (j + 1) * HEAD_DIM] = total
        cross_copy(q).start()

    for side in range(2):
        side_copy(side).start()
    for q in range(CHUNKS):
        spread(q)
    for k in range(2):
        result_copy(k).start()
        outs[k][:, mine] = (attended, grad_query)[k][pl.ds(pl.multiple_of(head * BLOCK, BLOCK), BLOCK)]
    runs[count] = jnp.zeros((ROWS, HEAD_DIM), F32)
    for q in range(CHUNKS):
        share(q)
    collect(0)
    collect(1)
    ring((0, 1))
    collect(2)
    collect(3)
    ring((2, 3))
    for side in range(2):
        side_copy(side).wait()
    for q in range(CHUNKS):
        finish(q)
    for q in range(CHUNKS):

        @pl.loop(1, PLANE)
        def _(i):
            shared_copy(q, i).wait_send()
            plane_copy(q, i).wait_send()

        for d in range(2):
            for t in range(ring_hops(q, d)):
                ring_copy(q, d, t).wait_send()
        cross_copy(q).wait()
    for k in range(2):
        result_copy(k).wait()


def give_back(c, picks, order, first, ends, shared_ends, attended, grad_query, own, sides, both, terms, collective_id):
    smem = pl.BlockSpec(memory_space=pltpu.SMEM)
    vmem = pl.BlockSpec(memory_space=pltpu.VMEM)
    dma = pltpu.SemaphoreType.DMA
    vm = pltpu.VMEM
    part = (PLANE * (c + 1), ROWS, HEAD_DIM)
    return pl.pallas_call(
        functools.partial(give_back_kernel, c),
        out_shape=(jax.ShapeDtypeStruct((BLOCK, 2 * WIDTH), BF16),) * 4,
        in_specs=[smem] * 5 + [vmem] * (5 + CHUNKS),
        out_specs=(vmem,) * 4,
        scratch_shapes=[vm(part, BF16)] * (2 * CHUNKS)
        + [vm((DEPTH * ITEMS, ROWS, HEAD_DIM), F32)] * CHUNKS
        + [vm((PLANE + 1, ROWS, HEAD_DIM), BF16)] * CHUNKS
        + [
            vm((CHUNKS, ROWS, HEAD_DIM), BF16),
            vm((PLANE * c + 1, ROWS, HEAD_DIM), F32),
            vm((7 * CHUNKS, ITEMS, ROWS, HEAD_DIM), BF16),
            vm((7 * CHUNKS, ITEMS, ROWS, HEAD_DIM), BF16),
            vm((2 * CHUNKS * HEADS_HERE, ROWS, HEAD_DIM), BF16),
            vm((CHUNKS, ROWS, WIDTH), BF16),
            dma((7 * CHUNKS,)),
            dma((7 * CHUNKS,)),
            dma((CHUNKS * PLANE,)),
            dma((CHUNKS * PLANE,)),
            dma((CHUNKS * PLANE,)),
            dma((CHUNKS * PLANE,)),
            dma((2,)),
            dma((2,)),
            dma((2 + CHUNKS,)),
            dma((2 + CHUNKS,)),
        ],
        compiler_params=pltpu.CompilerParams(
            collective_id=collective_id, has_side_effects=True, vmem_limit_bytes=VMEM_BYTES
        ),
        name=f"give_back_{c}",
    )(picks, order, first, ends, shared_ends, attended, grad_query, own, sides, both, *terms)


def on_device(
    query_vectors, key_vectors, value_vectors, cotangent, rand_peer, rand_local, global_ids
):
    seq = lax.axis_index("seq")
    column = seq % PLANE
    none = DEPTH * ITEMS
    peers = rand_peer[0].reshape(PICKS)
    heads = jnp.arange(HEADS_HERE, dtype=jnp.int32)
    inner = (rand_local[0] * HEADS_HERE + heads[None, :, None]).reshape(PICKS)
    items = (peers // PLANE) * ITEMS + inner
    columns = peers % PLANE
    numbers = jnp.arange(PICKS, dtype=jnp.int32)
    earlier = (columns[:, None] == columns[None, :]) & (numbers[None, :] < numbers[:, None])
    ranks = jnp.sum(earlier.astype(jnp.int32), axis=1)
    spots = columns * PLANE + ranks
    hits = spots[None, :] == jnp.arange(PLANE * PLANE, dtype=jnp.int32)[:, None]
    table = jnp.min(jnp.where(hits, items[None, :], none), axis=1).reshape(PLANE, PLANE)
    picks = jnp.max(jnp.where(hits, numbers[None, :], 0), axis=1).reshape(PLANE, PLANE)
    most = jnp.max(ranks) + 1
    lanes = jnp.arange(128, dtype=jnp.int32)
    padded = jnp.pad(table, ((0, 0), (0, 128 - PLANE)), constant_values=0)
    padded = jnp.where(lanes[None, :] == PLANE, most, padded)
    got, peaks = swap_tables(jnp.broadcast_to(padded[:, None, :], (PLANE, 8, 128)))
    asked = got[:, 0, :PLANE]
    peak = jnp.max(peaks[:, 0, PLANE])
    last_block = PLANE * DEPTH * BLOCKS_HERE - 1
    pair = jnp.stack([global_ids[0] + global_ids[1] - last_block, jnp.array(last_block, jnp.int32)])
    pair_peer = pair // BLOCKS_HERE
    pair_items = (pair_peer // PLANE) * ITEMS + (pair % BLOCKS_HERE) * HEADS_HERE
    pair_items = (pair_items[:, None] + heads[None, :]).reshape(PLANE)
    pair_columns = jnp.repeat(pair_peer % PLANE, HEADS_HERE)
    glob = jnp.concatenate([pair_items, pair_columns])
    all_items = jnp.arange(none, dtype=jnp.int32)
    here = (pair_items[None, :] == all_items[:, None]) & (pair_columns[None, :] == column)
    shared_ends = jnp.min(
        jnp.where(here, jnp.arange(PLANE, dtype=jnp.int32)[None, :], PLANE), axis=1
    )

    def path(c, ids):
        def run(query, key, value, grad):
            wanted = asked[:, :c]
            slots = jnp.where(wanted == none, 0, wanted)
            halo, shared, *picked = fetch(c, slots, glob, key, value, ids[0])
            where = columns * (c + 1) + ranks
            attended, grad_query, own, sides, both, *terms = attend(
                where, query, grad, key, value, halo, shared, picked
            )
            count = PLANE * c
            keys = wanted.reshape(count)
            at = jnp.arange(count, dtype=jnp.int32)
            before = (keys[None, :] < keys[:, None]) | (
                (keys[None, :] == keys[:, None]) & (at[None, :] < at[:, None])
            )
            sorted_at = jnp.sum(before.astype(jnp.int32), axis=1)
            chosen = sorted_at[None, :] == at[:, None]
            spot = (at // c) * (c + 1) + at % c
            order = jnp.sum(jnp.where(chosen, spot[None, :], 0), axis=1)
            opens = ~jnp.any((keys[None, :] == keys[:, None]) & (at[None, :] < at[:, None]), axis=1)
            first = jnp.sum(jnp.where(chosen & opens[None, :], 1, 0), axis=1)
            upto = jnp.sum((keys[None, :] <= all_items[:, None]).astype(jnp.int32), axis=1)
            found = jnp.any(keys[None, :] == all_items[:, None], axis=1)
            ends = jnp.where(found, upto - 1, count)
            return give_back(
                c, picks[:, :c], order, first, ends, shared_ends,
                attended, grad_query, own, sides, both, terms, ids[1],
            )

        return run

    return lax.cond(
        peak > 8, path(16, (3, 4)), path(8, (1, 2)),
        query_vectors, key_vectors, value_vectors, cotangent,
    )


def solution(mesh):
    placed = (
        P("seq", "head"),
        P("seq", "head"),
        P("seq", "head"),
        P("seq", "head"),
        P("head", "seq", None, None),
        P("head", "seq", None, None),
        P(),
    )
    return jax.shard_map(
        on_device,
        mesh=mesh,
        in_specs=placed,
        out_specs=(P(("seq", "head"), None),) * 4,
        check_vma=False,
    )
```

time: 765 us -> 268 us (0.35)
  waiting for transfers between devices: 493 us -> 0 us
  Pallas kernels: 0 us -> 251 us
  other arithmetic: 76.7 us -> 6.27 us
  starting transfers between devices: 53.2 us -> 0 us
  local copies, waits for them, and re-layouts: 58.7 us -> 7.21 us
  matrix products: 43.8 us -> 0 us
  between operations: 20.7 us -> 3.33 us
  blocking collectives: 16.4 us -> 0 us
    psum x2 -> x0, waiting for transfers between devices: 456 us -> none  [the longest x1 230 us: on_device(): global_total = lax.psum(global_terms, 'seq')]
    pallas_call x0 -> x4, Pallas kernels: none -> 251 us  [the longest x1 124 us: give_back(): pl.pallas_call(functools.partial(give_back_kernel, c), out_shape=(jax.Sha...]
    dot_general x38 -> x0, matrix products: 43.8 us -> none  [the longest x8 16.1 us: attend(): jnp.einsum('zta,zan->ztn', logit_gradient, block_key_rows, preferred_elem...]
    all_to_all x4 -> x0, starting transfers between devices: 43.6 us -> none  [the longest x1 16.3 us: on_device(): lax.all_to_all(ask_table.reshape(seq_count, slot_depth), 'seq', split_axi...]
    scatter-add x3 -> x0, other arithmetic: 34.4 us -> none  [the longest x1 33.2 us: on_device(): by_owner = jnp.zeros((head_count * blocks_here, 2, BLOCK, HEAD_DIM), jnp....]
    ppermute x4 -> x0, waiting for transfers between devices: 28.2 us -> none  [the longest x2 14.7 us: shifted(): lax.ppermute(value, axis, [(source, source + steps) for source in range(i...]
    select_n x5 -> x4, other arithmetic: 17.6 us -> 1.22 us  [the longest x1 0.6 us: run(): slots = jnp.where(wanted == none, 0, wanted)]
    all_to_all x3 -> x0, blocking collectives: 16.4 us -> none  [the longest x1 8.84 us: on_device(): lax.all_to_all(grad_value_rows, 'head', split_axis=0, concat_axis=1, tile...]
  transfers between devices with their start and end apart: 10 -> 0, of which waited for: 6 -> 0; matrix products, arithmetic and copies ran while one was open for 5% -> 0% of each run, Pallas kernels for 0% -> 0%
where the time goes in v1:
time: 268 us
  Pallas kernels  251 us (94%)
  local copies, waits for them, and re-layouts  7.21 us (3%)
  other arithmetic  6.27 us (2%)
  between operations  3.33 us (1%)
    pallas_call x1, Pallas kernels, give_back(): pl.pallas_call(functools.partial(give_back_kernel, c), out_shape=(jax.Sha...  124 us
    pallas_call x1, Pallas kernels, fetch(): pl.pallas_call(functools.partial(fetch_kernel, c), out_shape=(jax.ShapeDt...  93.7 us
    pallas_call x1, Pallas kernels, swap_tables(): pl.pallas_call(swap_tables_kernel, out_shape=(shape, shape), in_specs=[vm...  21.7 us
    pallas_call x1, Pallas kernels, attend(): pl.pallas_call(attend_kernel, out_shape=(rows, rows, jax.ShapeDtypeStruct...  11.5 us

profile of v1, /device:TPU:1, one launch (start us, length us, event | category | flops | bytes accessed | tf_op | source)
XLA Modules:
  0.0 267.7 jit_solution(11183668736479909151)
XLA Ops:
  0.6 1.3 fusion.16
  3.3 0.1 fusion.15
  3.4 0.1 broadcast_in_dim.145
  3.4 0.1 reshape.341
  3.5 0.1 iota_add_fusion
  3.6 0.1 add.183
  3.7 0.1 select_reduce_fusion.6
  3.8 0.7 broadcast_multiply_fusion
  4.5 0.1 copy.24
  4.6 0.1 mul.66
  4.7 0.1 add.174
  4.7 0.8 copy.23
  5.5 0.1 reshape_squeeze.2
  5.6 0.2 convert_reduce_fusion.4
  5.8 0.6 fusion.17
  6.4 0.1 select_reduce_fusion.4
  6.5 0.1 reshape.339
  7.3 0.6 broadcast_in_dim.142.table
  7.9 21.7 %swap_tables.1 = (s32[16,8,128]{2,1,0:T(8,128)}, s32[16,8,128]{2,1,0:T(8,128)}) custom-call(s32[16,8,128]{2,1,0:T(8,128)} %broadcast_in_dim.142.table), custom_call_target="tpu_custom_call" | custom-call | tf_op jit(solution)/shard_map/swap_tables/pallas_call | solution.py:102
  29.6 0.8 slice.19
  30.5 0.1 reshape.340
  30.5 0.1 pad_add_fusion.1
  30.6 1.6 slice_reduce_fusion
  32.8 232.0 %conditional.1 = ((bf16[64,2048]{1,0:T(8,128)(2,1)S(1)}, bf16[64,2048]{1,0:T(8,128)(2,1)S(1)}, bf16[64,2048]{1,0:T(8,128)(2,1)S(1)}, bf16[64,2048]{1,0:T(8,128)(2,1)S(1)})) conditional(s32[]{:T(128)} %convert_element_type.19, (s32[16,16]{1,0:T(8,128)S(1)}, s32[16,16]{1,0:T(8,128)S(1)}, s32[128]{0:T(128)S(1)}, s32[128]{0:T(128)S(1)}, ...), branch_computations={%region_6.13_spmd, %region_13.20_spmd} | conditional | flops 1281376 | bytes 20820 | solution.py:746
  32.9 0.6 compare_select_fusion
  33.5 93.7 %fetch_8.1 = (bf16[4,64,1024]{2,1,0:T(8,128)(2,1)}, bf16[64,32,128]{2,1,0:T(8,128)(2,1)}, bf16[144,32,128]{2,1,0:T(8,128)(2,1)}, bf16[144,32,128]{2,1,0:T(8,128)...) custom-call(s32[16,8]{1,0:T(8,128)} %get-tuple-element.135.slots, s32[32]{0:T(128)S(1)} %get-tuple-element.59.glob, ...), custom_call_target="tpu_custom_call" | custom-call | tf_op jit(solution)/shard_map/cond/branch_0_fun/fetch_8/pallas_call | solution.py:275
  127.2 0.5 multiply_add_fusion.where
  127.7 11.5 %attend.2 = (bf16[128,1024]{1,0:T(8,128)(2,1)}, bf16[128,1024]{1,0:T(8,128)(2,1)}, f32[64,32,128]{2,1,0:T(8,128)}, bf16[64,32,128]{2,1,0:T(8,128)(2,1)}, bf16[64...) custom-call(s32[48]{0:T(128)} %multiply_add_fusion.where, ...), custom_call_target="tpu_custom_call" | custom-call | tf_op jit(solution)/shard_map/cond/branch_0_fun/attend/pallas_call | solution.py:431
  139.2 0.1 lt.66
  139.3 0.2 compare_reduce_fusion
  139.5 0.2 convert_reduce_fusion
  139.7 0.6 select_reduce_fusion
  140.3 0.6 add_select_fusion.ends
  140.9 123.9 %give_back_8.1 = (bf16[64,2048]{1,0:T(8,128)(2,1)S(1)}, bf16[64,2048]{1,0:T(8,128)(2,1)S(1)}, bf16[64,2048]{1,0:T(8,128)(2,1)S(1)}, bf16[64,2048]{1,0:T(8,128)(2,1)S(1)}) custom-call(s32[16,8]{1,0:T(8,128)S(1)} %bitcast.9, s32[128]{0:T(128)} %get-tuple-element.128.order, s32[128]{0:T(128)} %get-tuple-element.127.first, s32[128]{0:T(128)} %add_select_fusion.ends, ...), custom_call_target="tpu_custom_call" | custom-call | tf_op jit(solution)/shard_map/cond/branch_0_fun/give_back_8/pallas_call | solution.py:644
  264.8 0.7 copy.37
  265.5 0.7 copy.38
  266.2 0.7 copy.39
  266.9 0.7 copy.40
  (10 shorter events, 0.1 us)

commit v2 on v1

v2 whole, which is shorter than its diff:
```python
import functools

import jax
import jax.numpy as jnp
from jax import lax
from jax.experimental import pallas as pl
from jax.experimental.pallas import tpu as pltpu
from jax.sharding import PartitionSpec as P

MESH = pl.DeviceIdType.MESH
HEAD_DIM = 128
BLOCK = 64
HEADS_HERE = 8
BLOCKS_HERE = 2
WIDTH = HEADS_HERE * HEAD_DIM
PLANE = 16
DEPTH = 8
ITEMS = BLOCKS_HERE * HEADS_HERE
PICKS = 3 * ITEMS
ROWS = 16
PARTS = BLOCK // ROWS
CHUNKS = 2 * PARTS
LANES = 32
FULL = PLANE + 1
USUAL = 8
VMEM_BYTES = 56 * 1024 * 1024
F32 = jnp.float32
BF16 = jnp.bfloat16


def position():
    seq = lax.axis_index("seq")
    return seq, lax.div(seq, PLANE), lax.rem(seq, PLANE), lax.axis_index("head")


def signal(seq, head):
    pl.semaphore_signal(
        pltpu.get_barrier_semaphore(), inc=1, device_id=(seq, head), device_id_type=MESH
    )


def remote(src, dst, send, recv, seq, head):
    return pltpu.make_async_remote_copy(
        src_ref=src,
        dst_ref=dst,
        send_sem=send,
        recv_sem=recv,
        device_id=(seq, head),
        device_id_type=MESH,
    )


def ring_hops(q, d):
    return 4 if (d == 0) == (q % 2 == 0) else 3


def ring_slot(q, d, t):
    return sum(ring_hops(q, e) for e in range(d)) + 7 * q + t


def fetch_kernel(c, glob, table, key, value, got, most, halo, shared, *rest):
    picked, held, out = rest[0:CHUNKS], rest[CHUNKS : 2 * CHUNKS], rest[2 * CHUNKS : 3 * CHUNKS]
    (
        relay, slots, local,
        zsend, zrecv, psend, precv, gsend, grecv, hsend, hrecv, tsend, trecv, msend, mrecv,
    ) = rest[3 * CHUNKS :]
    seq, z, p, head = position()
    place = z * 2 + head

    def table_copy(i):
        peer = lax.rem(p + i, PLANE)
        return remote(
            table.at[peer], got.at[p], tsend.at[i], trecv.at[i], z * PLANE + peer, head
        )

    def most_copy(i):
        other = lax.rem(place + i, 2 * DEPTH)
        return remote(
            most.at[place],
            most.at[place],
            msend.at[i],
            mrecv.at[i],
            lax.div(other, 2) * PLANE + p,
            lax.rem(other, 2),
        )

    def halo_copy(side, kv):
        block = (1 - side) * BLOCK
        other = lax.rem(seq + (1 if side == 0 else PLANE * DEPTH - 1), PLANE * DEPTH)
        return remote(
            (key, value)[kv].at[pl.ds(block, BLOCK)],
            halo.at[side * 2 + kv],
            hsend.at[side * 2 + kv],
            hrecv.at[side * 2 + kv],
            other,
            head,
        )

    def ring_copy(q, d, t):
        step = 1 if d == 0 else DEPTH - 1
        owner = lax.rem(z + t * (DEPTH - step), DEPTH)
        rows = pl.ds(owner * ITEMS, ITEMS)
        slot = ring_slot(q, d, t)
        return remote(
            held[q].at[rows],
            held[q].at[rows],
            zsend.at[slot],
            zrecv.at[slot],
            lax.rem(z + step, DEPTH) * PLANE + p,
            head,
        )

    def plane_copy(q, i):
        peer = lax.rem(p + i, PLANE)
        return remote(
            out[q].at[pl.ds(peer * c, c)],
            picked[q].at[pl.ds(p * c, c)],
            psend.at[q * PLANE + i],
            precv.at[q * PLANE + i],
            z * PLANE + peer,
            head,
        )

    def shared_copy(q, i):
        peer = lax.rem(p + i, PLANE)
        return remote(
            relay.at[q],
            shared.at[q * PLANE + p],
            gsend.at[q * PLANE + i],
            grecv.at[q * PLANE + i],
            z * PLANE + peer,
            head,
        )

    def fill(q):
        source, part = (key, value)[q // PARTS], q % PARTS
        for b in range(BLOCKS_HERE):
            for j in range(HEADS_HERE):
                held[q][z * ITEMS + b * HEADS_HERE + j] = source[
                    b * BLOCK + part * ROWS : b * BLOCK + (part + 1) * ROWS,
                    j * HEAD_DIM : (j + 1) * HEAD_DIM,
                ]

    def ring_start(q):
        for d in range(2):
            ring_copy(q, d, 0).start()

    def ring_step(q, t):
        for d in range(2):
            if t < ring_hops(q, d):
                ring_copy(q, d, t).wait_recv()
                if t + 1 < ring_hops(q, d):
                    ring_copy(q, d, t + 1).start()

    def spread(q):
        @pl.loop(1, PLANE)
        def _(i):
            peer = lax.rem(p + i, PLANE)
            for s in range(c):
                out[q][peer * c + s] = held[q][slots[peer, 0, s]]
            plane_copy(q, i).start()

        for s in range(c):
            picked[q][p * c + s] = held[q][slots[p, 0, s]]

    def share(q):
        @pl.loop(1, PLANE)
        def _(i):
            plane_copy(q, i).wait_recv()

        relay[q] = picked[q][glob[0]]
        shared[q * PLANE + p] = relay[q]

        @pl.loop(1, PLANE)
        def _(i):
            shared_copy(q, i).start()

    fill(0)

    @pl.loop(1, 2 * DEPTH)
    def _(i):
        other = lax.rem(place + i, 2 * DEPTH)
        signal(lax.div(other, 2) * PLANE + p, lax.rem(other, 2))

    @pl.loop(1, PLANE)
    def _(i):
        signal(z * PLANE + lax.rem(p + i, PLANE), head)

    for step in (1, PLANE * DEPTH - 1):
        signal(lax.rem(seq + step, PLANE * DEPTH), head)
    pl.semaphore_wait(pltpu.get_barrier_semaphore(), 2 * DEPTH - 1 + PLANE - 1 + 2)

    ring_start(0)

    @pl.loop(1, PLANE)
    def _(i):
        table_copy(i).start()

    got[p] = table[p]
    for q in range(1, CHUNKS):
        fill(q)
    for side in range(2):
        for kv in range(2):
            halo_copy(side, kv).start()

    ring_start(1)
    for step in range(CHUNKS + 4):
        for t in range(3, -1, -1):
            if 0 <= step - t < CHUNKS:
                ring_step(step - t, t)
        if step + 2 < CHUNKS:
            ring_start(step + 2)
        if step == 2:

            @pl.loop(1, PLANE)
            def _(i):
                table_copy(i).wait()

            to_scalars = pltpu.make_async_copy(got, slots, local)
            to_scalars.start()
            to_scalars.wait()
        if 0 <= step - 3 < CHUNKS:
            spread(step - 3)
        if step == 4:
            most[place] = jnp.max(got[...], axis=0)

            @pl.loop(1, 2 * DEPTH)
            def _(i):
                most_copy(i).start()

    for q in range(CHUNKS):
        share(q)

    @pl.loop(1, 2 * DEPTH)
    def _(i):
        most_copy(i).wait()

    for q in range(CHUNKS):

        @pl.loop(1, PLANE)
        def _(i):
            shared_copy(q, i).wait()
            plane_copy(q, i).wait_send()

        for d in range(2):
            for t in range(ring_hops(q, d)):
                ring_copy(q, d, t).wait_send()
    for side in range(2):
        for kv in range(2):
            halo_copy(side, kv).wait()


def fetch(c, glob, table, key, value, collective_id):
    smem = pl.BlockSpec(memory_space=pltpu.SMEM)
    vmem = pl.BlockSpec(memory_space=pltpu.VMEM)
    part = jax.ShapeDtypeStruct((PLANE * c, ROWS, HEAD_DIM), BF16)
    rows = jax.ShapeDtypeStruct((PLANE, 8, 128), jnp.int32)
    dma = pltpu.SemaphoreType.DMA
    return pl.pallas_call(
        functools.partial(fetch_kernel, c),
        out_shape=(
            rows,
            rows,
            jax.ShapeDtypeStruct((4, BLOCK, WIDTH), BF16),
            jax.ShapeDtypeStruct((CHUNKS * PLANE, ROWS, HEAD_DIM), BF16),
        )
        + (part,) * CHUNKS,
        in_specs=[smem, vmem, vmem, vmem],
        out_specs=(vmem,) * (4 + CHUNKS),
        scratch_shapes=[pltpu.VMEM((DEPTH * ITEMS, ROWS, HEAD_DIM), BF16)] * CHUNKS
        + [pltpu.VMEM(part.shape, BF16)] * CHUNKS
        + [
            pltpu.VMEM((CHUNKS, ROWS, HEAD_DIM), BF16),
            pltpu.SMEM((PLANE, 8, 128), jnp.int32),
            dma(()),
            dma((7 * CHUNKS,)),
            dma((7 * CHUNKS,)),
            dma((CHUNKS * PLANE,)),
            dma((CHUNKS * PLANE,)),
            dma((CHUNKS * PLANE,)),
            dma((CHUNKS * PLANE,)),
            dma((4,)),
            dma((4,)),
            dma((PLANE,)),
            dma((PLANE,)),
            dma((2 * DEPTH,)),
            dma((2 * DEPTH,)),
        ],
        compiler_params=pltpu.CompilerParams(
            collective_id=collective_id, has_side_effects=True, vmem_limit_bytes=VMEM_BYTES
        ),
        name=f"fetch_{c}",
    )(glob, table, key, value)


def dot(a, b, contract):
    return lax.dot_general(a, b, ((contract[0:1], contract[1:2]), ((), ())), preferred_element_type=F32)


def back_kernel(c, where, picks, order, first, ends, shared_ends, query, grad, key, value, halo, shared, *rest):
    picked, rest = rest[:CHUNKS], rest[CHUNKS:]
    outs, rest = rest[:4], rest[4:]
    terms, rest = rest[:CHUNKS], rest[CHUNKS:]
    out, rest = rest[:CHUNKS], rest[CHUNKS:]
    arrived, rest = rest[:CHUNKS], rest[CHUNKS:]
    totals, rest = rest[:CHUNKS], rest[CHUNKS:]
    gathered, rest = rest[:CHUNKS], rest[CHUNKS:]
    (
        attended, grad_query, own, sides, both, weights,
        relay, runs, zout, zin, beside, cross,
        zsend, zrecv, psend, precv, gsend, grecv, hsend, hrecv, csend, crecv,
    ) = rest
    seq, z, p, head = position()

    @pl.loop(1, PLANE)
    def _(i):
        signal(z * PLANE + lax.rem(p + i, PLANE), head)

    for step in (1, DEPTH - 1):
        signal(lax.rem(z + step, DEPTH) * PLANE + p, head)
    for step in (1, PLANE * DEPTH - 1):
        signal(lax.rem(seq + step, PLANE * DEPTH), head)
    signal(seq, 1 - head)

    scale = HEAD_DIM ** (-0.5)
    near = 4 * BLOCK
    rows = lax.broadcasted_iota(jnp.int32, (near, 128), 0)
    lanes = lax.broadcasted_iota(jnp.int32, (near, 128), 1)
    hidden = (
        ((lanes < BLOCK) & (rows >= 3 * BLOCK))
        | ((lanes >= BLOCK) & (rows < BLOCK))
        | ((rows < BLOCK) & (seq == 0))
        | ((rows >= 3 * BLOCK) & (seq == PLANE * DEPTH - 1))
    )
    pick_lanes = lax.broadcasted_iota(jnp.int32, (3 * BLOCK, 128), 1) < BLOCK

    def columns_of(j):
        return pl.ds(pl.multiple_of(j * HEAD_DIM, HEAD_DIM), HEAD_DIM)

    def listed(kv, j):
        cols = columns_of(j)
        close = [halo[kv, :, cols], (key, value)[kv][:, cols], halo[2 + kv, :, cols]]
        for group in range(2):
            for part in range(PARTS):
                close.append(shared[(kv * PARTS + part) * PLANE + group * HEADS_HERE + j])
        far = []
        for b in range(BLOCKS_HERE):
            pieces = []
            for t in range(3):
                at = where[b * 24 + j * 3 + t]
                for part in range(PARTS):
                    pieces.append(picked[kv * PARTS + part][at])
            far.append(jnp.concatenate(pieces, axis=0))
        return jnp.concatenate(close, axis=0), far

    def products(close, far, other):
        a = dot(close, other, (1, 1))
        b = jnp.where(pick_lanes, dot(far[0], other, (1, 1)), dot(far[1], other, (1, 1)))
        return a, b

    def gather(near_w, far_w, close, far):
        total = dot(near_w, close, (0, 0))
        top_rows = dot(far_w, far[0], (0, 0))
        low_rows = dot(far_w, far[1], (0, 0))
        return total + jnp.concatenate([top_rows[:BLOCK], low_rows[BLOCK:]], axis=0)

    def scatter(kv, j, weight_near, weight_far, rows_here):
        near_terms = dot(weight_near, rows_here, (1, 0))
        zero = jnp.zeros_like(weight_far)
        far_terms = (
            dot(jnp.where(pick_lanes, weight_far, zero), rows_here, (1, 0)).astype(BF16),
            dot(jnp.where(pick_lanes, zero, weight_far), rows_here, (1, 0)).astype(BF16),
        )
        for part in range(PARTS):
            chunk = kv * PARTS + part

            def piece(block):
                start = block * BLOCK + part * ROWS
                return near_terms[start : start + ROWS]

            sides[chunk * HEADS_HERE + j] = piece(0).astype(BF16)
            sides[(CHUNKS + chunk) * HEADS_HERE + j] = piece(3).astype(BF16)
            for b in range(BLOCKS_HERE):
                own[chunk * ITEMS + b * HEADS_HERE + j] = piece(1 + b)
                for t in range(3):
                    start = t * BLOCK + part * ROWS
                    terms[chunk][b * 24 + j * 3 + t] = far_terms[b][start : start + ROWS]
            for group in range(2):
                both[chunk * PLANE + group * HEADS_HERE + j] = piece(4 + group).astype(BF16)

    def weigh(j):
        cols = columns_of(j)
        keys, far_keys = listed(0, j)
        s_near, s_far = products(keys, far_keys, query[:, cols])
        s_near = s_near * scale
        s_far = s_far * scale
        s_near = jnp.concatenate(
            [jnp.where(hidden, -1e30, s_near[:near]), s_near[near:]], axis=0
        )
        top = jnp.maximum(
            jnp.max(s_near, axis=0, keepdims=True), jnp.max(s_far, axis=0, keepdims=True)
        )
        w_near = jnp.exp(s_near - top)
        w_far = jnp.exp(s_far - top)
        total = jnp.sum(w_near, axis=0, keepdims=True) + jnp.sum(w_far, axis=0, keepdims=True)
        inverse = 1.0 / total
        w_near = w_near * inverse
        w_far = w_far * inverse
        weights[j, : 6 * BLOCK] = w_near
        weights[j, 6 * BLOCK :] = w_far
        scatter(1, j, w_near.astype(BF16), w_far.astype(BF16), grad[:, cols])

    def backward(j):
        cols = columns_of(j)
        q, g = query[:, cols], grad[:, cols]
        keys, far_keys = listed(0, j)
        values, far_values = listed(1, j)
        w_near, w_far = weights[j, : 6 * BLOCK], weights[j, 6 * BLOCK :]
        gw_near, gw_far = products(values, far_values, g)
        centre = jnp.sum(w_near * gw_near, axis=0, keepdims=True) + jnp.sum(
            w_far * gw_far, axis=0, keepdims=True
        )
        d_near = (w_near * (gw_near - centre) * scale).astype(BF16)
        d_far = (w_far * (gw_far - centre) * scale).astype(BF16)
        scatter(0, j, d_near, d_far, q)
        attended[:, cols] = gather(
            w_near.astype(BF16), w_far.astype(BF16), values, far_values
        ).astype(BF16)
        grad_query[:, cols] = gather(d_near, d_far, keys, far_keys).astype(BF16)

    count = PLANE * c
    mine = pl.ds(pl.multiple_of(head * WIDTH, WIDTH), WIDTH)

    def result_copy(k):
        source = (attended, grad_query)[k].at[pl.ds((1 - head) * BLOCK, BLOCK)]
        return remote(source, outs[k].at[:, mine], csend.at[k], crecv.at[k], seq, 1 - head)

    def cross_copy(q):
        return remote(
            cross.at[q],
            outs[2 + q // PARTS].at[pl.ds((q % PARTS) * ROWS, ROWS), mine],
            csend.at[2 + q],
            crecv.at[2 + q],
            seq,
            1 - head,
        )

    def side_copy(kv, side):
        size = PARTS * HEADS_HERE
        other = lax.rem(seq + (PLANE * DEPTH - 1 if side == 0 else 1), PLANE * DEPTH)
        return remote(
            sides.at[pl.ds((side * 2 + kv) * size, size)],
            beside.at[pl.ds(((1 - side) * 2 + kv) * size, size)],
            hsend.at[kv * 2 + side],
            hrecv.at[kv * 2 + side],
            other,
            head,
        )

    def plane_copy(q, i):
        peer = lax.rem(p + i, PLANE)
        return remote(
            out[q].at[pl.ds(peer * (c + 1), c + 1)],
            arrived[q].at[pl.ds(p * (c + 1), c + 1)],
            psend.at[q * PLANE + i],
            precv.at[q * PLANE + i],
            z * PLANE + peer,
            head,
        )

    def shared_copy(q, i):
        peer = lax.rem(p + i, PLANE)
        return remote(
            relay.at[q],
            gathered[q].at[p],
            gsend.at[q * PLANE + i],
            grecv.at[q * PLANE + i],
            z * PLANE + peer,
            head,
        )

    def shared_out(i):
        return (p < HEADS_HERE) | (lax.rem(p + i, PLANE) == PLANE - 1)

    def shared_in(i):
        return (lax.rem(p + PLANE - i, PLANE) < HEADS_HERE) | (p == PLANE - 1)

    def ring_copy(q, d, t):
        step = 1 if d == 0 else DEPTH - 1
        slot = ring_slot(q, d, t)
        return remote(
            zout.at[slot],
            zin.at[slot],
            zsend.at[slot],
            zrecv.at[slot],
            lax.rem(z + step, DEPTH) * PLANE + p,
            head,
        )

    def spread(q):
        @pl.loop(1, PLANE)
        def _(i):
            peer = lax.rem(p + i, PLANE)
            for s in range(c):
                out[q][peer * (c + 1) + s] = terms[q][picks[peer, s]]
            out[q][peer * (c + 1) + c] = both[q * PLANE + peer]
            plane_copy(q, i).start()

        for s in range(c):
            arrived[q][p * (c + 1) + s] = terms[q][picks[p, s]]
        arrived[q][p * (c + 1) + c] = both[q * PLANE + p]

    def share(q):
        @pl.loop(1, PLANE)
        def _(i):
            plane_copy(q, i).wait_recv()

        total = arrived[q][c].astype(F32)
        for i in range(1, PLANE):
            total = total + arrived[q][i * (c + 1) + c].astype(F32)
        relay[q] = total.astype(BF16)
        gathered[q][p] = relay[q]
        gathered[q][PLANE] = jnp.zeros((ROWS, HEAD_DIM), BF16)

        @pl.loop(1, PLANE)
        def _(i):
            @pl.when(shared_out(i))
            def _():
                shared_copy(q, i).start()

    def collect(q):
        def add(r, total):
            term = arrived[q][order[r]].astype(F32)
            total = jnp.where(first[r] == 1, term, total + term)
            runs[r] = total
            return total

        lax.fori_loop(0, count, add, jnp.zeros((ROWS, HEAD_DIM), F32), unroll=8)

        @pl.loop(1, PLANE)
        def _(i):
            @pl.when(shared_in(i))
            def _():
                shared_copy(q, i).wait_recv()

        @pl.loop(0, DEPTH * ITEMS, unroll=8)
        def _(i):
            totals[q][i] = runs[ends[i]] + gathered[q][shared_ends[i]].astype(F32)

    def ring_step(q, t):
        for d in range(2):
            hops = ring_hops(q, d)
            if t < hops:
                away = hops - t
                target = lax.rem(z + (away if d == 0 else DEPTH - away), DEPTH)
                partial = totals[q][pl.ds(target * ITEMS, ITEMS)]
                if t > 0:
                    ring_copy(q, d, t - 1).wait_recv()
                    partial = partial + zin[ring_slot(q, d, t - 1)].astype(F32)
                zout[ring_slot(q, d, t)] = partial.astype(BF16)
                ring_copy(q, d, t).start()

    def finish(q):
        for d in range(2):
            ring_copy(q, d, ring_hops(q, d) - 1).wait_recv()
        kv, part = q // PARTS, q % PARTS
        for j in range(HEADS_HERE):
            for stays in range(2):
                b = head if stays else 1 - head
                item = b * HEADS_HERE + j
                total = totals[q][z * ITEMS + item] + own[q * ITEMS + item]
                total = total + beside[(b * CHUNKS + q) * HEADS_HERE + j].astype(F32)
                for d in range(2):
                    total = total + zin[ring_slot(q, d, ring_hops(q, d) - 1), item].astype(F32)
                total = total.astype(BF16)
                if stays:
                    cols = pl.ds(pl.multiple_of(head * WIDTH + j * HEAD_DIM, HEAD_DIM), HEAD_DIM)
                    outs[2 + kv][part * ROWS : (part + 1) * ROWS, cols] = total
                else:
                    cross[q, :, j * HEAD_DIM : (j + 1) * HEAD_DIM] = total
        cross_copy(q).start()

    @pl.loop(0, HEADS_HERE)
    def _(j):
        weigh(j)

    runs[count] = jnp.zeros((ROWS, HEAD_DIM), F32)
    pl.semaphore_wait(pltpu.get_barrier_semaphore(), PLANE + 4)
    turn = list(range(PARTS, CHUNKS)) + list(range(PARTS))
    spread(turn[0])
    spread(turn[1])
    for side in range(2):
        side_copy(1, side).start()

    @pl.loop(0, HEADS_HERE)
    def _(j):
        backward(j)

    for k in range(2):
        result_copy(k).start()
        outs[k][:, mine] = (attended, grad_query)[k][pl.ds(pl.multiple_of(head * BLOCK, BLOCK), BLOCK)]
    for side in range(2):
        side_copy(0, side).start()
    for step in range(CHUNKS + 6):
        if step + 2 < CHUNKS:
            spread(turn[step + 2])
        for t in range(3, 0, -1):
            if 0 <= step - 1 - t < CHUNKS:
                ring_step(turn[step - 1 - t], t)
        if 0 <= step - 1 < CHUNKS:
            collect(turn[step - 1])
            ring_step(turn[step - 1], 0)
        if step < CHUNKS:
            share(turn[step])
        if 0 <= step - 5 < CHUNKS:
            q = turn[step - 5]
            if q % PARTS == 0:
                for side in range(2):
                    side_copy(q // PARTS, side).wait()
            finish(q)
    for q in range(CHUNKS):

        @pl.loop(1, PLANE)
        def _(i):
            @pl.when(shared_out(i))
            def _():
                shared_copy(q, i).wait_send()

            plane_copy(q, i).wait_send()

        for d in range(2):
            for t in range(ring_hops(q, d)):
                ring_copy(q, d, t).wait_send()
        cross_copy(q).wait()
    for k in range(2):
        result_copy(k).wait()


def back(c, scalars, arrays, picked, collective_id):
    smem = pl.BlockSpec(memory_space=pltpu.SMEM)
    vmem = pl.BlockSpec(memory_space=pltpu.VMEM)
    dma = pltpu.SemaphoreType.DMA
    vm = pltpu.VMEM
    tile = (ROWS, HEAD_DIM)
    part = (PLANE * (c + 1),) + tile
    return pl.pallas_call(
        functools.partial(back_kernel, c),
        out_shape=(jax.ShapeDtypeStruct((BLOCK, 2 * WIDTH), BF16),) * 4,
        in_specs=[smem] * len(scalars) + [vmem] * (len(arrays) + CHUNKS),
        out_specs=(vmem,) * 4,
        scratch_shapes=[vm((PICKS,) + tile, BF16)] * CHUNKS
        + [vm(part, BF16)] * (2 * CHUNKS)
        + [vm((DEPTH * ITEMS,) + tile, F32)] * CHUNKS
        + [vm((PLANE + 1,) + tile, BF16)] * CHUNKS
        + [
            vm((BLOCKS_HERE * BLOCK, WIDTH), BF16),
            vm((BLOCKS_HERE * BLOCK, WIDTH), BF16),
            vm((CHUNKS * ITEMS,) + tile, F32),
            vm((2 * CHUNKS * HEADS_HERE,) + tile, BF16),
            vm((CHUNKS * PLANE,) + tile, BF16),
            vm((HEADS_HERE, 9 * BLOCK, 128), F32),
            vm((CHUNKS,) + tile, BF16),
            vm((PLANE * c + 1,) + tile, F32),
            vm((7 * CHUNKS, ITEMS) + tile, BF16),
            vm((7 * CHUNKS, ITEMS) + tile, BF16),
            vm((2 * CHUNKS * HEADS_HERE,) + tile, BF16),
            vm((CHUNKS, ROWS, WIDTH), BF16),
            dma((7 * CHUNKS,)),
            dma((7 * CHUNKS,)),
            dma((CHUNKS * PLANE,)),
            dma((CHUNKS * PLANE,)),
            dma((CHUNKS * PLANE,)),
            dma((CHUNKS * PLANE,)),
            dma((4,)),
            dma((4,)),
            dma((2 + CHUNKS,)),
            dma((2 + CHUNKS,)),
        ],
        compiler_params=pltpu.CompilerParams(
            collective_id=collective_id, has_side_effects=True, vmem_limit_bytes=VMEM_BYTES
        ),
        name=f"back_{c}",
    )(*scalars, *arrays, *picked)


def on_device(
    query_vectors, key_vectors, value_vectors, cotangent, rand_peer, rand_local, global_ids
):
    seq = lax.axis_index("seq")
    column = seq % PLANE
    none = DEPTH * ITEMS
    heads = jnp.arange(HEADS_HERE, dtype=jnp.int32)
    last_block = PLANE * DEPTH * BLOCKS_HERE - 1
    pair = jnp.stack([global_ids[0] + global_ids[1] - last_block, jnp.array(last_block, jnp.int32)])
    pair_peer = pair // BLOCKS_HERE
    pair_items = (pair_peer // PLANE) * ITEMS + (pair % BLOCKS_HERE) * HEADS_HERE
    pair_items = (pair_items[:, None] + heads[None, :]).reshape(PLANE)
    pair_columns = jnp.repeat(pair_peer % PLANE, HEADS_HERE)
    peers = rand_peer[0].reshape(PICKS)
    inner = (rand_local[0] * HEADS_HERE + heads[None, :, None]).reshape(PICKS)
    items = (peers // PLANE) * ITEMS + inner
    relayed = jnp.arange(PLANE, dtype=jnp.int32) == column
    relay_item = jnp.sum(jnp.where(relayed, pair_items, 0))
    relay_column = jnp.sum(jnp.where(relayed, pair_columns, 0))
    items = jnp.concatenate([items, relay_item[None]])
    columns = jnp.concatenate([peers % PLANE, relay_column[None]])
    numbers = jnp.arange(PICKS + 1, dtype=jnp.int32)
    earlier = (columns[:, None] == columns[None, :]) & (numbers[None, :] < numbers[:, None])
    ranks = jnp.sum(earlier.astype(jnp.int32), axis=1)
    spots = columns * LANES + ranks
    hits = spots[None, :] == jnp.arange(PLANE * LANES, dtype=jnp.int32)[:, None]
    back_hits = hits & (numbers[None, :] < PICKS)
    table = jnp.max(jnp.where(hits, items[None, :], 0), axis=1).reshape(PLANE, LANES)
    back_keys = jnp.min(jnp.where(back_hits, items[None, :], none), axis=1).reshape(PLANE, LANES)
    picks = jnp.max(jnp.where(back_hits, numbers[None, :], 0), axis=1).reshape(PLANE, LANES)
    most = jnp.broadcast_to(jnp.max(ranks) + 1, (PLANE, LANES))
    padded = jnp.concatenate(
        [table, most, back_keys, jnp.zeros((PLANE, 128 - 3 * LANES), jnp.int32)], axis=1
    )
    padded = jnp.broadcast_to(padded[:, None, :], (PLANE, 8, 128))
    all_items = jnp.arange(none, dtype=jnp.int32)
    here = (pair_items[None, :] == all_items[:, None]) & (pair_columns[None, :] == column)
    shared_ends = jnp.min(
        jnp.where(here, jnp.arange(PLANE, dtype=jnp.int32)[None, :], PLANE), axis=1
    )

    def go(c, collective_id, key, value):
        at = jnp.minimum(relay_column * c + ranks[PICKS], PLANE * c - 1)[None]
        return fetch(c, at, padded, key, value, collective_id)

    def finish(c, collective_id, query, key, value, grad, fetched):
        got, _, halo, shared, *picked = fetched
        where = columns * c + ranks
        count = PLANE * c
        keys = got[:, 0, 2 * LANES : 2 * LANES + c].reshape(count)
        at = jnp.arange(count, dtype=jnp.int32)
        same = keys[None, :] == keys[:, None]
        ahead = at[None, :] < at[:, None]
        before = (keys[None, :] < keys[:, None]) | (same & ahead)
        sorted_at = jnp.sum(before.astype(jnp.int32), axis=1)
        chosen = sorted_at[None, :] == at[:, None]
        spot = (at // c) * (c + 1) + at % c
        order = jnp.sum(jnp.where(chosen, spot[None, :], 0), axis=1)
        opens = ~jnp.any(same & ahead, axis=1)
        first = jnp.sum(jnp.where(chosen & opens[None, :], 1, 0), axis=1)
        upto = jnp.sum((keys[None, :] <= all_items[:, None]).astype(jnp.int32), axis=1)
        found = jnp.any(keys[None, :] == all_items[:, None], axis=1)
        ends = jnp.where(found, upto - 1, count)
        return back(
            c,
            (where, picks[:, :c], order, first, ends, shared_ends),
            (query, grad, key, value, halo, shared),
            picked,
            collective_id,
        )

    def usual(query, key, value, grad, *fetched):
        return finish(USUAL, 1, query, key, value, grad, fetched)

    def crowded(query, key, value, grad, *fetched):
        return finish(FULL, 3, query, key, value, grad, go(FULL, 2, key, value))

    fetched = go(USUAL, 0, key_vectors, value_vectors)
    peak = jnp.max(fetched[1][:, 0, LANES])
    return lax.cond(
        peak > USUAL, crowded, usual,
        query_vectors, key_vectors, value_vectors, cotangent, *fetched,
    )


def solution(mesh):
    placed = (
        P("seq", "head"),
        P("seq", "head"),
        P("seq", "head"),
        P("seq", "head"),
        P("head", "seq", None, None),
        P("head", "seq", None, None),
        P(),
    )
    return jax.shard_map(
        on_device,
        mesh=mesh,
        in_specs=placed,
        out_specs=(P(("seq", "head"), None),) * 4,
        check_vma=False,
    )
```

time: 268 us -> 221 us (0.82)
  Pallas kernels: 251 us -> 200 us
    pallas_call x4 -> x2, Pallas kernels: 251 us -> 200 us  [the longest x1 107 us: back(): pl.pallas_call(functools.partial(back_kernel, c), out_shape=(jax.ShapeDty...]
where the time goes in v2:
time: 221 us
  Pallas kernels  200 us (90%)
  other arithmetic  8.35 us (4%)
  local copies, waits for them, and re-layouts  8.22 us (4%)
  between operations  4.64 us (2%)
    pallas_call x1, Pallas kernels, back(): pl.pallas_call(functools.partial(back_kernel, c), out_shape=(jax.ShapeDty...  107 us
    pallas_call x1, Pallas kernels, fetch(): pl.pallas_call(functools.partial(fetch_kernel, c), out_shape=(rows, rows,...  92 us
    unnamed x9, local copies, waits for them, and re-layouts  4.56 us

profile of v2, /device:TPU:1, one launch (start us, length us, event | category | flops | bytes accessed | tf_op | source)
XLA Modules:
  0.0 220.9 jit_solution(7900052631482488017)
XLA Ops:
  0.7 0.1 pad.3.clone
  0.7 0.6 iota.85
  1.3 1.3 fusion.23
  3.9 0.1 broadcast_compare_fusion
  4.0 0.1 broadcast_in_dim.156
  4.1 0.1 eq.154
  4.2 0.7 iota_add_fusion
  5.6 0.1 add.172
  5.7 0.1 select_reduce_fusion.7
  5.8 0.7 broadcast_multiply_fusion
  6.4 0.1 copy.26
  6.5 0.1 mul.70
  6.6 0.8 copy.25
  7.4 0.1 reshape_squeeze.3
  7.5 0.1 add.163
  7.6 0.7 pad_add_fusion.2
  8.3 0.7 pad_add_fusion.1
  9.0 0.2 convert_reduce_fusion.4
  9.2 0.6 slice.29
  10.5 1.3 fusion.22
  12.4 0.1 pad.1.clone
  12.5 0.1 select_reduce_fusion.4
  12.6 0.1 reshape.264
  12.7 0.1 reshape.263
  12.8 0.1 reshape.262
  12.9 0.1 add_add_fusion
  12.9 92.0 %fetch_8.1 = (s32[16,8,128]{2,1,0:T(8,128)S(1)}, s32[16,8,128]{2,1,0:T(8,128)}, bf16[4,64,1024]{2,1,0:T(8,128)(2,1)S(1)}, bf16[128,16,128]{2,1,0:T(8,128)(2,1)S(...) custom-call(s32[1]{0:T(128)} %bitcast.4.glob, ...), custom_call_target="tpu_custom_call" | custom-call | tf_op jit(solution)/shard_map/fetch_8/pallas_call | solution.py:259
  105.0 1.6 slice_reduce_fusion.1
  107.2 109.9 %conditional.1 = ((bf16[64,2048]{1,0:T(8,128)(2,1)S(1)}, bf16[64,2048]{1,0:T(8,128)(2,1)}, bf16[64,2048]{1,0:T(8,128)(2,1)}, bf16[64,2048]{1,0:T(8,128)(2,1)})) conditional(s32[]{:T(128)} %convert_element_type.19, (s32[49]{0:T(128)S(1)}, s32[49]{0:T(128)S(1)}, s32[16,32]{1,0:T(8,128)S(1)}, s32[16,8,128]{2,1,0:T(8,128)S(1)}, s32[128]{0:T(128)S(1)}, ...), branch_computations={%region_9.16_spmd, %region_16.23_spmd} | conditional | flops 1434901 | bytes 141140 | solution.py:765
  107.2 0.5 multiply_add_fusion.where
  107.7 0.1 slice.31
  107.8 0.1 lt.66
  107.9 0.2 convert_reduce_fusion
  108.1 0.2 compare_reduce_fusion
  108.3 0.5 add_select_fusion.ends
  108.8 0.6 select_reduce_fusion
  109.4 107.5 %back_8.1 = (bf16[64,2048]{1,0:T(8,128)(2,1)S(1)}, bf16[64,2048]{1,0:T(8,128)(2,1)}, bf16[64,2048]{1,0:T(8,128)(2,1)}, bf16[64,2048]{1,0:T(8,128)(2,1)}) custom-call(s32[49]{0:T(128)} %multiply_add_fusion.where, s32[16,8]{1,0:T(8,128)S(1)} %bitcast.14, s32[128]{0:T(128)} %get-tuple-element.216.order, s32[128]{0:T(128)} %get-tuple-element.215.first, ...), custom_call_target="tpu_custom_call" | custom-call | tf_op jit(solution)/shard_map/cond/branch_0_fun/back_8/pallas_call | solution.py:646
  217.1 0.0 copy-start
  217.1 0.0 copy-start.1
  217.1 0.7 copy.40
  217.9 1.7 copy.41
  219.5 0.0 copy-done
  219.5 0.7 copy.42
  220.2 0.0 copy-done.1
  220.2 0.7 copy.43
  (11 shorter events, 0.1 us)
Async XLA Ops:
  217.1 2.4 %copy-start = (bf16[64,2048]{1,0:T(8,128)(2,1)S(1)}, bf16[64,2048]{1,0:T(8,128)(2,1)}, u32[]{:S(2)}) copy-start(bf16[64,2048]{1,0:T(8,128)(2,1)} %get-tuple-element.249) | copy-start | bytes 786436
  217.1 3.1 %copy-start.1 = (bf16[64,2048]{1,0:T(8,128)(2,1)S(1)}, bf16[64,2048]{1,0:T(8,128)(2,1)}, u32[]{:S(2)}) copy-start(bf16[64,2048]{1,0:T(8,128)(2,1)} %get-tuple-element.250) | copy-start | bytes 786436

commit v3 on v2

--- a/solution.py
+++ b/solution.py
@@ -21,8 +21,9 @@
 PARTS = BLOCK // ROWS
 CHUNKS = 2 * PARTS
 LANES = 32
-FULL = PLANE + 1
+FULL = 2 * DEPTH
 USUAL = 8
+LAST_BLOCK = PLANE * DEPTH * BLOCKS_HERE - 1
 VMEM_BYTES = 56 * 1024 * 1024
 F32 = jnp.float32
 BF16 = jnp.bfloat16
@@ -58,10 +59,58 @@
     return sum(ring_hops(q, e) for e in range(d)) + 7 * q + t
 
 
-def fetch_kernel(c, glob, table, key, value, got, most, halo, shared, *rest):
-    picked, held, out = rest[0:CHUNKS], rest[CHUNKS : 2 * CHUNKS], rest[2 * CHUNKS : 3 * CHUNKS]
+def global_block(ids, e):
+    return jnp.where(e < HEADS_HERE, ids[0] + ids[1] - LAST_BLOCK, LAST_BLOCK)
+
+
+def global_place(ids, e):
+    block = global_block(ids, e)
+    peer = block >> 1
+    plane = peer >> 4
+    item = plane * ITEMS + (block & 1) * HEADS_HERE + lax.rem(e, HEADS_HERE)
+    return plane, peer & (PLANE - 1), item
+
+
+def write_tables(c, rand_peer, rand_local, table, where, plan):
+    shape = (PICKS, 128)
+    number = lax.broadcasted_iota(jnp.int32, shape, 0)
+    lane = lax.broadcasted_iota(jnp.int32, shape, 1)
+
+    def spread_out(ref):
+        parts = []
+        for t in range(3):
+            for b in range(BLOCKS_HERE):
+                parts.append(jnp.broadcast_to(ref[0, b][:, t : t + 1], (HEADS_HERE, 128)))
+        return jnp.concatenate(parts, axis=0)
+
+    peer, spot = spread_out(rand_peer), spread_out(rand_local)
+    column = peer & (PLANE - 1)
+    item = (peer >> 4) * ITEMS + spot * HEADS_HERE + (number & (HEADS_HERE - 1))
+    along = jnp.sum(jnp.where(number == lane, column, 0), axis=0, keepdims=True)
+    ahead = (column == along) & (lane < number)
+    rank = jnp.sum(jnp.where(ahead, 1, 0), axis=1, keepdims=True)
+    rank = jnp.broadcast_to(rank, shape)
+    most = jnp.max(rank, axis=0, keepdims=True) + 1
+    where[...] = jnp.minimum(column * c + rank, PLANE * c - 1)
+    group = lane >> 5
+    none = DEPTH * ITEMS
+    worth = jnp.where(group == 0, item, 0)
+    worth = jnp.where(group == 2, item - none, worth)
+    worth = jnp.where(group == 3, number, worth)
+    here = rank == (lane & (LANES - 1))
+    row_group = group[0:1]
+    rest = jnp.where(row_group == 2, none, jnp.where(row_group == 1, most, 0))
+    for col in range(PLANE):
+        line = jnp.sum(jnp.where(here & (column == col), worth, 0), axis=0, keepdims=True)
+        line = line + rest
+        table[col] = jnp.broadcast_to(line, (8, 128))
+        plan[col : col + 1, :] = line
+
+
+def fetch_kernel(c, ids, rand_peer, rand_local, key, value, got, peak, where, plan, halo, shared, *rest):
+    picked, held, out = rest[0:CHUNKS], rest[CHUNKS : 2 * CHUNKS] + (shared,), rest[2 * CHUNKS : 3 * CHUNKS]
     (
-        relay, slots, local,
+        relay, offer, offered, piece, pieces, slots, table, most, local,
         zsend, zrecv, psend, precv, gsend, grecv, hsend, hrecv, tsend, trecv, msend, mrecv,
     ) = rest[3 * CHUNKS :]
     seq, z, p, head = position()
@@ -121,16 +170,104 @@
             head,
         )
 
-    def shared_copy(q, i):
+    def offer_copy(i):
         peer = lax.rem(p + i, PLANE)
         return remote(
-            relay.at[q],
-            shared.at[q * PLANE + p],
-            gsend.at[q * PLANE + i],
-            grecv.at[q * PLANE + i],
+            offer.at[pl.ds(peer * CHUNKS, CHUNKS)],
+            offered.at[pl.ds(p * CHUNKS, CHUNKS)],
+            gsend.at[i],
+            grecv.at[i],
             z * PLANE + peer,
             head,
         )
+
+    def piece_copy(i):
+        other = lax.rem(z + i, DEPTH)
+        return remote(
+            piece.at[other],
+            pieces.at[z],
+            gsend.at[PLANE + i],
+            grecv.at[PLANE + i],
+            other * PLANE + p,
+            head,
+        )
+
+    def relay_copy(i):
+        return remote(
+            relay,
+            shared.at[z * PLANE + p],
+            gsend.at[PLANE + DEPTH + i],
+            grecv.at[PLANE + DEPTH + i],
+            z * PLANE + lax.rem(p + i, PLANE),
+            head,
+        )
+
+    def offers(sender, peer):
+        return (peer < HEADS_HERE) | (sender == PLANE - 1)
+
+    def offer_start():
+        for e in range(PLANE):
+            second = (global_block(ids, e) & 1) == 1
+            j = e % HEADS_HERE
+            for q in range(CHUNKS):
+                low, high = [
+                    (key, value)[q // PARTS][
+                        b * BLOCK + (q % PARTS) * ROWS : b * BLOCK + (q % PARTS + 1) * ROWS,
+                        j * HEAD_DIM : (j + 1) * HEAD_DIM,
+                    ]
+                    for b in range(BLOCKS_HERE)
+                ]
+                offer[e * CHUNKS + q] = jnp.where(second, high, low)
+
+        @pl.loop(1, PLANE)
+        def _(i):
+            @pl.when(offers(p, lax.rem(p + i, PLANE)))
+            def _():
+                offer_copy(i).start()
+
+        mine = pl.ds(p * CHUNKS, CHUNKS)
+        offered[mine] = offer[mine]
+
+    def piece_start():
+        @pl.loop(1, PLANE)
+        def _(i):
+            @pl.when(offers(lax.rem(p + PLANE - i, PLANE), p))
+            def _():
+                offer_copy(i).wait_recv()
+
+        _, column, _ = global_place(ids, p)
+        for q in range(CHUNKS):
+            found = offered[(PLANE - 1) * CHUNKS + q]
+            for source in range(PLANE - 1):
+                found = jnp.where(column == source, offered[source * CHUNKS + q], found)
+            piece[q] = found
+
+        @pl.loop(1, DEPTH)
+        def _(i):
+            piece_copy(i).start()
+
+        pieces[z] = piece[z]
+
+    def relay_start():
+        @pl.loop(1, DEPTH)
+        def _(i):
+            piece_copy(i).wait_recv()
+
+        plane, _, _ = global_place(ids, p)
+        found = pieces[DEPTH - 1]
+        for source in range(DEPTH - 1):
+            found = jnp.where(plane == source, pieces[source], found)
+        relay[...] = found
+        shared[z * PLANE + p] = relay[...]
+
+        @pl.loop(1, PLANE)
+        def _(i):
+            relay_copy(i).start()
+
+    def relay_wait():
+        @pl.loop(1, PLANE)
+        def _(i):
+            relay_copy(i).wait_recv()
 
     def fill(q):
         source, part = (key, value)[q // PARTS], q % PARTS
@@ -163,18 +300,6 @@
         for s in range(c):
             picked[q][p * c + s] = held[q][slots[p, 0, s]]
 
-    def share(q):
-        @pl.loop(1, PLANE)
-        def _(i):
-            plane_copy(q, i).wait_recv()
-
-        relay[q] = picked[q][glob[0]]
-        shared[q * PLANE + p] = relay[q]
-
-        @pl.loop(1, PLANE)
-        def _(i):
-            shared_copy(q, i).start()
-
     fill(0)
 
     @pl.loop(1, 2 * DEPTH)
@@ -191,25 +316,34 @@
     pl.semaphore_wait(pltpu.get_barrier_semaphore(), 2 * DEPTH - 1 + PLANE - 1 + 2)
 
     ring_start(0)
+    fill(1)
+    ring_start(1)
+    write_tables(c, rand_peer, rand_local, table, where, plan)
 
     @pl.loop(1, PLANE)
     def _(i):
         table_copy(i).start()
 
     got[p] = table[p]
-    for q in range(1, CHUNKS):
+    offer_start()
+    for q in range(2, CHUNKS):
         fill(q)
     for side in range(2):
         for kv in range(2):
             halo_copy(side, kv).start()
 
-    ring_start(1)
     for step in range(CHUNKS + 4):
         for t in range(3, -1, -1):
-            if 0 <= step - t < CHUNKS:
+            if 0 <= step - t <= CHUNKS:
                 ring_step(step - t, t)
-        if step + 2 < CHUNKS:
+        if step + 2 == CHUNKS:
+            relay_wait()
+        if step + 2 <= CHUNKS:
             ring_start(step + 2)
+        if step == 1:
+            piece_start()
+        if step == 3:
+            relay_start()
         if step == 2:
 
             @pl.loop(1, PLANE)
@@ -228,19 +362,29 @@
             def _(i):
                 most_copy(i).start()
 
-    for q in range(CHUNKS):
-        share(q)
-
     @pl.loop(1, 2 * DEPTH)
     def _(i):
         most_copy(i).wait()
 
-    for q in range(CHUNKS):
-
-        @pl.loop(1, PLANE)
-        def _(i):
-            shared_copy(q, i).wait()
-            plane_copy(q, i).wait_send()
+    peak[...] = jnp.max(most[...], axis=0)
+    @pl.loop(1, PLANE)
+    def _(i):
+        @pl.when(offers(p, lax.rem(p + i, PLANE)))
+        def _():
+            offer_copy(i).wait_send()
+
+        relay_copy(i).wait_send()
+
+    @pl.loop(1, DEPTH)
+    def _(i):
+        piece_copy(i).wait_send()
+
+    for q in range(CHUNKS + 1):
+        if q < CHUNKS:
+
+            @pl.loop(1, PLANE)
+            def _(i):
+                plane_copy(q, i).wait()
 
         for d in range(2):
             for t in range(ring_hops(q, d)):
@@ -250,7 +394,7 @@
             halo_copy(side, kv).wait()
 
 
-def fetch(c, glob, table, key, value, collective_id):
+def fetch(c, ids, rand_peer, rand_local, key, value, collective_id):
     smem = pl.BlockSpec(memory_space=pltpu.SMEM)
     vmem = pl.BlockSpec(memory_space=pltpu.VMEM)
     part = jax.ShapeDtypeStruct((PLANE * c, ROWS, HEAD_DIM), BF16)
@@ -260,25 +404,33 @@
         functools.partial(fetch_kernel, c),
         out_shape=(
             rows,
-            rows,
+            jax.ShapeDtypeStruct((8, 128), jnp.int32),
+            jax.ShapeDtypeStruct((PICKS, 128), jnp.int32),
+            jax.ShapeDtypeStruct((PLANE, 128), jnp.int32),
             jax.ShapeDtypeStruct((4, BLOCK, WIDTH), BF16),
             jax.ShapeDtypeStruct((CHUNKS * PLANE, ROWS, HEAD_DIM), BF16),
         )
         + (part,) * CHUNKS,
-        in_specs=[smem, vmem, vmem, vmem],
-        out_specs=(vmem,) * (4 + CHUNKS),
+        in_specs=[smem, vmem, vmem, vmem, vmem],
+        out_specs=(vmem,) * (6 + CHUNKS),
         scratch_shapes=[pltpu.VMEM((DEPTH * ITEMS, ROWS, HEAD_DIM), BF16)] * CHUNKS
         + [pltpu.VMEM(part.shape, BF16)] * CHUNKS
         + [
-            pltpu.VMEM((CHUNKS, ROWS, HEAD_DIM), BF16),
+            pltpu.VMEM((ROWS, HEAD_DIM), BF16),
+            pltpu.VMEM((PLANE * CHUNKS, ROWS, HEAD_DIM), BF16),
+            pltpu.VMEM((PLANE * CHUNKS, ROWS, HEAD_DIM), BF16),
+            pltpu.VMEM((DEPTH, ROWS, HEAD_DIM), BF16),
+            pltpu.VMEM((DEPTH, ROWS, HEAD_DIM), BF16),
             pltpu.SMEM((PLANE, 8, 128), jnp.int32),
+            pltpu.VMEM((PLANE, 8, 128), jnp.int32),
+            pltpu.VMEM((2 * DEPTH, 8, 128), jnp.int32),
             dma(()),
-            dma((7 * CHUNKS,)),
-            dma((7 * CHUNKS,)),
+            dma((7 * (CHUNKS + 1),)),
+            dma((7 * (CHUNKS + 1),)),
             dma((CHUNKS * PLANE,)),
             dma((CHUNKS * PLANE,)),
-            dma((CHUNKS * PLANE,)),
-            dma((CHUNKS * PLANE,)),
+            dma((2 * PLANE + DEPTH,)),
+            dma((2 * PLANE + DEPTH,)),
             dma((4,)),
             dma((4,)),
             dma((PLANE,)),
@@ -290,24 +442,23 @@
             collective_id=collective_id, has_side_effects=True, vmem_limit_bytes=VMEM_BYTES
         ),
         name=f"fetch_{c}",
-    )(glob, table, key, value)
+    )(ids, rand_peer, rand_local, key, value)
 
 
 def dot(a, b, contract):
     return lax.dot_general(a, b, ((contract[0:1], contract[1:2]), ((), ())), preferred_element_type=F32)
 
 
-def back_kernel(c, where, picks, order, first, ends, shared_ends, query, grad, key, value, halo, shared, *rest):
+def back_kernel(c, ids, where, plan, order, first, ends, query, grad, key, value, halo, shared, *rest):
     picked, rest = rest[:CHUNKS], rest[CHUNKS:]
     outs, rest = rest[:4], rest[4:]
     terms, rest = rest[:CHUNKS], rest[CHUNKS:]
     out, rest = rest[:CHUNKS], rest[CHUNKS:]
     arrived, rest = rest[:CHUNKS], rest[CHUNKS:]
     totals, rest = rest[:CHUNKS], rest[CHUNKS:]
-    gathered, rest = rest[:CHUNKS], rest[CHUNKS:]
     (
         attended, grad_query, own, sides, both, weights,
-        relay, runs, zout, zin, beside, cross,
+        zone_in, zone, tile_in, tile_total, relay, runs, zout, zin, beside, cross,
         zsend, zrecv, psend, precv, gsend, grecv, hsend, hrecv, csend, crecv,
     ) = rest
     seq, z, p, head = position()
@@ -316,8 +467,10 @@
     def _(i):
         signal(z * PLANE + lax.rem(p + i, PLANE), head)
 
-    for step in (1, DEPTH - 1):
-        signal(lax.rem(z + step, DEPTH) * PLANE + p, head)
+    @pl.loop(1, DEPTH)
+    def _(i):
+        signal(lax.rem(z + i, DEPTH) * PLANE + p, head)
+
     for step in (1, PLANE * DEPTH - 1):
         signal(lax.rem(seq + step, PLANE * DEPTH), head)
     signal(seq, 1 - head)
@@ -347,7 +500,7 @@
         for b in range(BLOCKS_HERE):
             pieces = []
             for t in range(3):
-                at = where[b * 24 + j * 3 + t]
+                at = where[t * ITEMS + b * HEADS_HERE + j, 0]
                 for part in range(PARTS):
                     pieces.append(picked[kv * PARTS + part][at])
             far.append(jnp.concatenate(pieces, axis=0))
@@ -384,9 +537,9 @@
                 own[chunk * ITEMS + b * HEADS_HERE + j] = piece(1 + b)
                 for t in range(3):
                     start = t * BLOCK + part * ROWS
-                    terms[chunk][b * 24 + j * 3 + t] = far_terms[b][start : start + ROWS]
+                    terms[chunk][t * ITEMS + b * HEADS_HERE + j] = far_terms[b][start : start + ROWS]
             for group in range(2):
-                both[chunk * PLANE + group * HEADS_HERE + j] = piece(4 + group).astype(BF16)
+                both[((kv * 2 + group) * HEADS_HERE + j) * PARTS + part] = piece(4 + group).astype(BF16)
 
     def weigh(j):
         cols = columns_of(j)
@@ -460,30 +613,98 @@
     def plane_copy(q, i):
         peer = lax.rem(p + i, PLANE)
         return remote(
-            out[q].at[pl.ds(peer * (c + 1), c + 1)],
-            arrived[q].at[pl.ds(p * (c + 1), c + 1)],
+            out[q].at[pl.ds(peer * c, c)],
+            arrived[q].at[pl.ds(p * c, c)],
             psend.at[q * PLANE + i],
             precv.at[q * PLANE + i],
             z * PLANE + peer,
             head,
         )
 
-    def shared_copy(q, i):
+    def zone_copy(kv, i):
+        other = lax.rem(z + i, DEPTH)
+        rows = pl.ds((kv * PLANE + other * 2) * PARTS, 2 * PARTS)
+        return remote(
+            both.at[rows],
+            zone_in.at[pl.ds((kv * DEPTH + z) * 2 * PARTS, 2 * PARTS)],
+            gsend.at[kv * DEPTH + i],
+            grecv.at[kv * DEPTH + i],
+            other * PLANE + p,
+            head,
+        )
+
+    def tile_copy(kv, i):
         peer = lax.rem(p + i, PLANE)
         return remote(
-            relay.at[q],
-            gathered[q].at[p],
-            gsend.at[q * PLANE + i],
-            grecv.at[q * PLANE + i],
+            zone.at[kv * 2 * PARTS + lax.rem(peer, 2 * PARTS)],
+            tile_in.at[p],
+            gsend.at[2 * DEPTH + i],
+            grecv.at[2 * DEPTH + i],
             z * PLANE + peer,
             head,
         )
 
-    def shared_out(i):
-        return (p < HEADS_HERE) | (lax.rem(p + i, PLANE) == PLANE - 1)
-
-    def shared_in(i):
-        return (lax.rem(p + PLANE - i, PLANE) < HEADS_HERE) | (p == PLANE - 1)
+    def total_copy(i):
+        peer = lax.rem(p + i, PLANE)
+        return remote(
+            relay,
+            tile_total.at[p],
+            gsend.at[2 * DEPTH + PLANE + i],
+            grecv.at[2 * DEPTH + PLANE + i],
+            z * PLANE + peer,
+            head,
+        )
+
+    def adds(kv, q):
+        return lax.div(q, 2 * PARTS) == 1 - kv
+
+    def zone_start(kv):
+        @pl.loop(1, DEPTH)
+        def _(i):
+            zone_copy(kv, i).start()
+
+    def zone_add(kv):
+        @pl.loop(1, DEPTH)
+        def _(i):
+            zone_copy(kv, i).wait_recv()
+
+        size = 2 * PARTS
+        total = both[pl.ds((kv * PLANE + z * 2) * PARTS, size)].astype(F32)
+        for i in range(1, DEPTH):
+            other = lax.rem(z + i, DEPTH)
+            total = total + zone_in[pl.ds((kv * DEPTH + other) * size, size)].astype(F32)
+        zone[kv * size : (kv + 1) * size] = total.astype(BF16)
+
+        @pl.loop(1, PLANE)
+        def _(i):
+            @pl.when(adds(kv, lax.rem(p + i, PLANE)))
+            def _():
+                tile_copy(kv, i).start()
+
+    def tile_add(kv):
+        @pl.when(adds(kv, p))
+        def _():
+            @pl.loop(1, PLANE)
+            def _(i):
+                tile_copy(kv, i).wait_recv()
+
+            tile_in[p] = zone[kv * 2 * PARTS + lax.rem(p, 2 * PARTS)]
+            total = tile_in[0].astype(F32)
+            for i in range(1, PLANE):
+                total = total + tile_in[i].astype(F32)
+            relay[...] = total.astype(BF16)
+            tile_total[p] = relay[...]
+
+            @pl.loop(1, PLANE)
+            def _(i):
+                total_copy(i).start()
+
+    def total_wait(kv):
+        @pl.loop(1, PLANE)
+        def _(i):
+            @pl.when(adds(kv, lax.rem(p + PLANE - i, PLANE)))
+            def _():
+                total_copy(i).wait_recv()
 
     def ring_copy(q, d, t):
         step = 1 if d == 0 else DEPTH - 1
@@ -502,33 +723,17 @@
         def _(i):
             peer = lax.rem(p + i, PLANE)
             for s in range(c):
-                out[q][peer * (c + 1) + s] = terms[q][picks[peer, s]]
-            out[q][peer * (c + 1) + c] = both[q * PLANE + peer]
+                out[q][peer * c + s] = terms[q][plan[peer, 3 * LANES + s]]
             plane_copy(q, i).start()
 
         for s in range(c):
-            arrived[q][p * (c + 1) + s] = terms[q][picks[p, s]]
-        arrived[q][p * (c + 1) + c] = both[q * PLANE + p]
-
-    def share(q):
+            arrived[q][p * c + s] = terms[q][plan[p, 3 * LANES + s]]
+
+    def collect(q):
         @pl.loop(1, PLANE)
         def _(i):
             plane_copy(q, i).wait_recv()
 
-        total = arrived[q][c].astype(F32)
-        for i in range(1, PLANE):
-            total = total + arrived[q][i * (c + 1) + c].astype(F32)
-        relay[q] = total.astype(BF16)
-        gathered[q][p] = relay[q]
-        gathered[q][PLANE] = jnp.zeros((ROWS, HEAD_DIM), BF16)
-
-        @pl.loop(1, PLANE)
-        def _(i):
-            @pl.when(shared_out(i))
-            def _():
-                shared_copy(q, i).start()
-
-    def collect(q):
         def add(r, total):
             term = arrived[q][order[r]].astype(F32)
             total = jnp.where(first[r] == 1, term, total + term)
@@ -536,16 +741,23 @@
             return total
 
         lax.fori_loop(0, count, add, jnp.zeros((ROWS, HEAD_DIM), F32), unroll=8)
-
-        @pl.loop(1, PLANE)
-        def _(i):
-            @pl.when(shared_in(i))
-            def _():
-                shared_copy(q, i).wait_recv()
+        kv, part = q // PARTS, q % PARTS
+        if part == 0:
+            total_wait(kv)
+        extra = [
+            tile_total[(1 - kv) * 2 * PARTS + e * PARTS + part].astype(F32) for e in range(2)
+        ]
+        spots = []
+        for e in range(2):
+            _, column, item = global_place(ids, z * 2 + e)
+            spots.append(jnp.where(column == p, item, -1))
 
         @pl.loop(0, DEPTH * ITEMS, unroll=8)
         def _(i):
-            totals[q][i] = runs[ends[i]] + gathered[q][shared_ends[i]].astype(F32)
+            total = runs[ends[i]]
+            for e in range(2):
+                total = total + jnp.where(spots[e] == i, extra[e], 0.0)
+            totals[q][i] = total
 
     def ring_step(q, t):
         for d in range(2):
@@ -585,47 +797,67 @@
         weigh(j)
 
     runs[count] = jnp.zeros((ROWS, HEAD_DIM), F32)
-    pl.semaphore_wait(pltpu.get_barrier_semaphore(), PLANE + 4)
+    pl.semaphore_wait(pltpu.get_barrier_semaphore(), PLANE + DEPTH + 1)
     turn = list(range(PARTS, CHUNKS)) + list(range(PARTS))
+    zone_start(1)
+    for side in range(2):
+        side_copy(1, side).start()
     spread(turn[0])
     spread(turn[1])
-    for side in range(2):
-        side_copy(1, side).start()
 
     @pl.loop(0, HEADS_HERE)
     def _(j):
         backward(j)
 
+    zone_add(1)
+    spread(turn[2])
+    zone_start(0)
+    for side in range(2):
+        side_copy(0, side).start()
     for k in range(2):
         result_copy(k).start()
         outs[k][:, mine] = (attended, grad_query)[k][pl.ds(pl.multiple_of(head * BLOCK, BLOCK), BLOCK)]
-    for side in range(2):
-        side_copy(0, side).start()
-    for step in range(CHUNKS + 6):
-        if step + 2 < CHUNKS:
+    for step in range(CHUNKS + 5):
+        if 0 < step and step + 2 < CHUNKS:
             spread(turn[step + 2])
+        if step == 0:
+            tile_add(1)
+        if step == 1:
+            zone_add(0)
+        if step == 3:
+            tile_add(0)
         for t in range(3, 0, -1):
-            if 0 <= step - 1 - t < CHUNKS:
-                ring_step(turn[step - 1 - t], t)
-        if 0 <= step - 1 < CHUNKS:
-            collect(turn[step - 1])
-            ring_step(turn[step - 1], 0)
+            if 0 <= step - t < CHUNKS:
+                ring_step(turn[step - t], t)
         if step < CHUNKS:
-            share(turn[step])
-        if 0 <= step - 5 < CHUNKS:
-            q = turn[step - 5]
+            collect(turn[step])
+            ring_step(turn[step], 0)
+        if 0 <= step - 4 < CHUNKS:
+            q = turn[step - 4]
             if q % PARTS == 0:
                 for side in range(2):
                     side_copy(q // PARTS, side).wait()
             finish(q)
+    for kv in range(2):
+
+        @pl.loop(1, DEPTH)
+        def _(i):
+            zone_copy(kv, i).wait_send()
+
+        @pl.loop(1, PLANE)
+        def _(i):
+            @pl.when(adds(kv, lax.rem(p + i, PLANE)))
+            def _():
+                tile_copy(kv, i).wait_send()
+
+    @pl.loop(1, PLANE)
+    def _(i):
+        total_copy(i).wait_send()
+
     for q in range(CHUNKS):
 
         @pl.loop(1, PLANE)
         def _(i):
-            @pl.when(shared_out(i))
-            def _():
-                shared_copy(q, i).wait_send()
-
             plane_copy(q, i).wait_send()
 
         for d in range(2):
@@ -642,7 +874,7 @@
     dma = pltpu.SemaphoreType.DMA
     vm = pltpu.VMEM
     tile = (ROWS, HEAD_DIM)
-    part = (PLANE * (c + 1),) + tile
+    part = (PLANE * c,) + tile
     return pl.pallas_call(
         functools.partial(back_kernel, c),
         out_shape=(jax.ShapeDtypeStruct((BLOCK, 2 * WIDTH), BF16),) * 4,
@@ -651,7 +883,6 @@
         scratch_shapes=[vm((PICKS,) + tile, BF16)] * CHUNKS
         + [vm(part, BF16)] * (2 * CHUNKS)
         + [vm((DEPTH * ITEMS,) + tile, F32)] * CHUNKS
-        + [vm((PLANE + 1,) + tile, BF16)] * CHUNKS
         + [
             vm((BLOCKS_HERE * BLOCK, WIDTH), BF16),
             vm((BLOCKS_HERE * BLOCK, WIDTH), BF16),
@@ -659,7 +890,11 @@
             vm((2 * CHUNKS * HEADS_HERE,) + tile, BF16),
             vm((CHUNKS * PLANE,) + tile, BF16),
             vm((HEADS_HERE, 9 * BLOCK, 128), F32),
-            vm((CHUNKS,) + tile, BF16),
+            vm((2 * DEPTH * 2 * PARTS,) + tile, BF16),
+            vm((2 * 2 * PARTS,) + tile, BF16),
+            vm((PLANE,) + tile, BF16),
+            vm((PLANE,) + tile, BF16),
+            vm(tile, BF16),
             vm((PLANE * c + 1,) + tile, F32),
             vm((7 * CHUNKS, ITEMS) + tile, BF16),
             vm((7 * CHUNKS, ITEMS) + tile, BF16),
@@ -669,8 +904,8 @@
             dma((7 * CHUNKS,)),
             dma((CHUNKS * PLANE,)),
             dma((CHUNKS * PLANE,)),
-            dma((CHUNKS * PLANE,)),
-            dma((CHUNKS * PLANE,)),
+            dma((2 * DEPTH + 2 * PLANE,)),
+            dma((2 * DEPTH + 2 * PLANE,)),
             dma((4,)),
             dma((4,)),
             dma((2 + CHUNKS,)),
@@ -686,51 +921,14 @@
 def on_device(
     query_vectors, key_vectors, value_vectors, cotangent, rand_peer, rand_local, global_ids
 ):
-    seq = lax.axis_index("seq")
-    column = seq % PLANE
     none = DEPTH * ITEMS
-    heads = jnp.arange(HEADS_HERE, dtype=jnp.int32)
-    last_block = PLANE * DEPTH * BLOCKS_HERE - 1
-    pair = jnp.stack([global_ids[0] + global_ids[1] - last_block, jnp.array(last_block, jnp.int32)])
-    pair_peer = pair // BLOCKS_HERE
-    pair_items = (pair_peer // PLANE) * ITEMS + (pair % BLOCKS_HERE) * HEADS_HERE
-    pair_items = (pair_items[:, None] + heads[None, :]).reshape(PLANE)
-    pair_columns = jnp.repeat(pair_peer % PLANE, HEADS_HERE)
-    peers = rand_peer[0].reshape(PICKS)
-    inner = (rand_local[0] * HEADS_HERE + heads[None, :, None]).reshape(PICKS)
-    items = (peers // PLANE) * ITEMS + inner
-    relayed = jnp.arange(PLANE, dtype=jnp.int32) == column
-    relay_item = jnp.sum(jnp.where(relayed, pair_items, 0))
-    relay_column = jnp.sum(jnp.where(relayed, pair_columns, 0))
-    items = jnp.concatenate([items, relay_item[None]])
-    columns = jnp.concatenate([peers % PLANE, relay_column[None]])
-    numbers = jnp.arange(PICKS + 1, dtype=jnp.int32)
-    earlier = (columns[:, None] == columns[None, :]) & (numbers[None, :] < numbers[:, None])
-    ranks = jnp.sum(earlier.astype(jnp.int32), axis=1)
-    spots = columns * LANES + ranks
-    hits = spots[None, :] == jnp.arange(PLANE * LANES, dtype=jnp.int32)[:, None]
-    back_hits = hits & (numbers[None, :] < PICKS)
-    table = jnp.max(jnp.where(hits, items[None, :], 0), axis=1).reshape(PLANE, LANES)
-    back_keys = jnp.min(jnp.where(back_hits, items[None, :], none), axis=1).reshape(PLANE, LANES)
-    picks = jnp.max(jnp.where(back_hits, numbers[None, :], 0), axis=1).reshape(PLANE, LANES)
-    most = jnp.broadcast_to(jnp.max(ranks) + 1, (PLANE, LANES))
-    padded = jnp.concatenate(
-        [table, most, back_keys, jnp.zeros((PLANE, 128 - 3 * LANES), jnp.int32)], axis=1
-    )
-    padded = jnp.broadcast_to(padded[:, None, :], (PLANE, 8, 128))
     all_items = jnp.arange(none, dtype=jnp.int32)
-    here = (pair_items[None, :] == all_items[:, None]) & (pair_columns[None, :] == column)
-    shared_ends = jnp.min(
-        jnp.where(here, jnp.arange(PLANE, dtype=jnp.int32)[None, :], PLANE), axis=1
-    )
-
-    def go(c, collective_id, key, value):
-        at = jnp.minimum(relay_column * c + ranks[PICKS], PLANE * c - 1)[None]
-        return fetch(c, at, padded, key, value, collective_id)
+
+    def go(c, collective_id, peers, spots, key, value):
+        return fetch(c, global_ids, peers, spots, key, value, collective_id)
 
     def finish(c, collective_id, query, key, value, grad, fetched):
-        got, _, halo, shared, *picked = fetched
-        where = columns * c + ranks
+        got, _, where, plan, halo, shared, *picked = fetched
         count = PLANE * c
         keys = got[:, 0, 2 * LANES : 2 * LANES + c].reshape(count)
         at = jnp.arange(count, dtype=jnp.int32)
@@ -739,8 +937,7 @@
         before = (keys[None, :] < keys[:, None]) | (same & ahead)
         sorted_at = jnp.sum(before.astype(jnp.int32), axis=1)
         chosen = sorted_at[None, :] == at[:, None]
-        spot = (at // c) * (c + 1) + at % c
-        order = jnp.sum(jnp.where(chosen, spot[None, :], 0), axis=1)
+        order = jnp.sum(jnp.where(chosen, at[None, :], 0), axis=1)
         opens = ~jnp.any(same & ahead, axis=1)
         first = jnp.sum(jnp.where(chosen & opens[None, :], 1, 0), axis=1)
         upto = jnp.sum((keys[None, :] <= all_items[:, None]).astype(jnp.int32), axis=1)
@@ -748,23 +945,22 @@
         ends = jnp.where(found, upto - 1, count)
         return back(
             c,
-            (where, picks[:, :c], order, first, ends, shared_ends),
+            (global_ids, where, plan, order, first, ends),
             (query, grad, key, value, halo, shared),
             picked,
             collective_id,
         )
 
-    def usual(query, key, value, grad, *fetched):
+    def usual(query, key, value, grad, peers, spots, *fetched):
         return finish(USUAL, 1, query, key, value, grad, fetched)
 
-    def crowded(query, key, value, grad, *fetched):
-        return finish(FULL, 3, query, key, value, grad, go(FULL, 2, key, value))
-
-    fetched = go(USUAL, 0, key_vectors, value_vectors)
-    peak = jnp.max(fetched[1][:, 0, LANES])
+    def crowded(query, key, value, grad, peers, spots, *fetched):
+        return finish(FULL, 3, query, key, value, grad, go(FULL, 2, peers, spots, key, value))
+
+    fetched = go(USUAL, 0, rand_peer, rand_local, key_vectors, value_vectors)
     return lax.cond(
-        peak > USUAL, crowded, usual,
-        query_vectors, key_vectors, value_vectors, cotangent, *fetched,
+        fetched[1][0, LANES] > USUAL, crowded, usual,
+        query_vectors, key_vectors, value_vectors, cotangent, rand_peer, rand_local, *fetched,
     )
 
 

time: 221 us -> 193 us (0.87)
  Pallas kernels: 200 us -> 182 us
  other arithmetic: 8.35 us -> 1.53 us
  between operations: 4.64 us -> 1.36 us
    pallas_call x1, Pallas kernels: 107 us -> 98.4 us  [back(): pl.pallas_call(functools.partial(back_kernel, c), out_shape=(jax.ShapeDty...]
    pallas_call x1, Pallas kernels: 92 us -> 84 us  [fetch(): pl.pallas_call(functools.partial(fetch_kernel, c), out_shape=(rows, jax.S...]
    reduce_max x3 -> x0, other arithmetic: 2.99 us -> none  [the longest x1 1.56 us: on_device(): peak = jnp.max(fetched[1][:, 0, LANES])]
    unnamed x9 -> x22, local copies, waits for them, and re-layouts: 4.56 us -> 5.87 us
where the time goes in v3:
time: 193 us
  Pallas kernels  182 us (94%)
  local copies, waits for them, and re-layouts  7.31 us (4%)
    pallas_call x1, Pallas kernels, back(): pl.pallas_call(functools.partial(back_kernel, c), out_shape=(jax.ShapeDty...  98.4 us
    pallas_call x1, Pallas kernels, fetch(): pl.pallas_call(functools.partial(fetch_kernel, c), out_shape=(rows, jax.S...  84 us
    unnamed x22, local copies, waits for them, and re-layouts  5.87 us

profile of v3, /device:TPU:1, one launch (start us, length us, event | category | flops | bytes accessed | tf_op | source)
XLA Modules:
  0.0 192.8 jit_solution(8414592892205531296)
XLA Ops:
  0.6 0.0 copy-start.7
  0.7 0.7 copy-done.7
  1.3 0.0 copy-start.8
  1.3 0.7 copy.29.rand_peer
  2.0 0.0 copy-done.8
  2.0 0.0 copy-start.9
  2.0 0.7 copy.30.rand_local
  2.7 0.0 copy-done.9
  2.7 0.0 copy-start
  2.7 0.0 copy-start.1
  2.7 84.0 %fetch_8.1 = (s32[16,8,128]{2,1,0:T(8,128)S(1)}, s32[8,128]{1,0:T(8,128)}, s32[48,128]{1,0:T(8,128)S(1)}, s32[16,128]{1,0:T(8,128)S(1)}, bf16[4,64,1024]{2,1,0:T...) custom-call(s32[2]{0:T(128)S(1)} %copy-done.9, ...), custom_call_target="tpu_custom_call" | custom-call | tf_op jit(solution)/shard_map/fetch_8/pallas_call | solution.py:403
  86.7 1.3 slice.9
  88.6 0.0 copy-done
  88.7 0.0 copy-done.1
  88.7 100.3 %conditional.1 = ((bf16[64,2048]{1,0:T(8,128)(2,1)S(1)}, bf16[64,2048]{1,0:T(8,128)(2,1)}, bf16[64,2048]{1,0:T(8,128)(2,1)}, bf16[64,2048]{1,0:T(8,128)(2,1)})) conditional(s32[]{:T(128)} %bitcast, (s32[16,8,128]{2,1,0:T(8,128)S(1)}, s32[128]{0:T(128)S(1)}, s32[128]{0:T(128)S(1)}, s32[2]{0:T(128)S(1)}, s32[48,128]{1,0:T(8,128)S(1)}, ...), branch_computations={%region_0.7_spmd, %region_7.14_spmd} | conditional | flops 1277184 | bytes 2114112 | solution.py:961
  88.7 0.1 slice.10
  88.8 0.1 lt.5
  88.9 0.2 convert_reduce_fusion
  89.1 0.2 compare_reduce_fusion
  89.2 0.5 add_select_fusion.ends
  89.8 0.6 select_reduce_fusion
  90.4 98.4 %back_8.1 = (bf16[64,2048]{1,0:T(8,128)(2,1)S(1)}, bf16[64,2048]{1,0:T(8,128)(2,1)}, bf16[64,2048]{1,0:T(8,128)(2,1)}, bf16[64,2048]{1,0:T(8,128)(2,1)}) custom-call(s32[2]{0:T(128)S(1)} %get-tuple-element.44.ids, s32[48,128]{1,0:T(8,128)S(1)} %get-tuple-element.45.where, s32[16,128]{1,0:T(8,128)S(1)} %get-tuple-element.58.plan, ...), custom_call_target="tpu_custom_call" | custom-call | tf_op jit(solution)/shard_map/cond/branch_0_fun/back_8/pallas_call | solution.py:878
  189.0 0.0 copy-start.4
  189.0 0.7 copy.46
  189.7 0.3 copy-done.4
  190.1 0.0 copy-start.5
  190.1 0.7 copy.47
  190.8 0.3 copy-done.5
  191.1 0.0 copy-start.6
  191.1 0.7 copy.48
  191.8 0.3 copy-done.6
  192.1 0.7 copy.49
  (4 shorter events, 0.0 us)
Async XLA Ops:
  0.6 0.7 copy-start.7
  1.3 0.7 copy-start.8
  2.0 0.7 copy-start.9
  2.7 85.9 %copy-start = (bf16[128,1024]{1,0:T(8,128)(2,1)S(1)}, bf16[128,1024]{1,0:T(8,128)(2,1)}, u32[]{:S(2)}) copy-start(bf16[128,1024]{1,0:T(8,128)(2,1)} %key.1) | copy-start | bytes 786436
  2.7 86.0 %copy-start.1 = (bf16[128,1024]{1,0:T(8,128)(2,1)S(1)}, bf16[128,1024]{1,0:T(8,128)(2,1)}, u32[]{:S(2)}) copy-start(bf16[128,1024]{1,0:T(8,128)(2,1)} %value.1) | copy-start | bytes 786436
  189.0 1.0 copy-start.4
  190.1 1.0 copy-start.5
  191.1 1.0 copy-start.6

commit v4 on v3

--- a/solution.py
+++ b/solution.py
@@ -22,9 +22,12 @@
 CHUNKS = 2 * PARTS
 LANES = 32
 FULL = 2 * DEPTH
+FEW = 7
 USUAL = 8
+SCALE = HEAD_DIM ** (-0.5)
 LAST_BLOCK = PLANE * DEPTH * BLOCKS_HERE - 1
-VMEM_BYTES = 56 * 1024 * 1024
+VMEM_FULL = 56 * 1024 * 1024
+VMEM_USUAL = 44 * 1024 * 1024
 F32 = jnp.float32
 BF16 = jnp.bfloat16
 
@@ -71,19 +74,17 @@
     return plane, peer & (PLANE - 1), item
 
 
-def write_tables(c, rand_peer, rand_local, table, where, plan):
+def write_tables(c, chosen, table, where, plan):
     shape = (PICKS, 128)
     number = lax.broadcasted_iota(jnp.int32, shape, 0)
     lane = lax.broadcasted_iota(jnp.int32, shape, 1)
 
-    def spread_out(ref):
-        parts = []
-        for t in range(3):
-            for b in range(BLOCKS_HERE):
-                parts.append(jnp.broadcast_to(ref[0, b][:, t : t + 1], (HEADS_HERE, 128)))
-        return jnp.concatenate(parts, axis=0)
-
-    peer, spot = spread_out(rand_peer), spread_out(rand_local)
+    parts = []
+    for t in range(3):
+        for b in range(BLOCKS_HERE):
+            parts.append(jnp.broadcast_to(chosen[0, b][:, t : t + 1], (HEADS_HERE, 128)))
+    block = jnp.concatenate(parts, axis=0)
+    peer, spot = block >> 1, block & 1
     column = peer & (PLANE - 1)
     item = (peer >> 4) * ITEMS + spot * HEADS_HERE + (number & (HEADS_HERE - 1))
     along = jnp.sum(jnp.where(number == lane, column, 0), axis=0, keepdims=True)
@@ -107,10 +108,13 @@
         plan[col : col + 1, :] = line
 
 
-def fetch_kernel(c, ids, rand_peer, rand_local, key, value, got, peak, where, plan, halo, shared, *rest):
+def fetch_kernel(
+    c, ids, chosen, key, value, query, grad, got, peak, where, plan, halo, shared, weights, own, sides, both, *rest
+):
+    terms, rest = rest[:PARTS], rest[PARTS:]
     picked, held, out = rest[0:CHUNKS], rest[CHUNKS : 2 * CHUNKS] + (shared,), rest[2 * CHUNKS : 3 * CHUNKS]
     (
-        relay, offer, offered, piece, pieces, slots, table, most, local,
+        relay, offer, offered, piece, pieces, slots, spots, table, most, local, local2,
         zsend, zrecv, psend, precv, gsend, grecv, hsend, hrecv, tsend, trecv, msend, mrecv,
     ) = rest[3 * CHUNKS :]
     seq, z, p, head = position()
@@ -318,7 +322,9 @@
     ring_start(0)
     fill(1)
     ring_start(1)
-    write_tables(c, rand_peer, rand_local, table, where, plan)
+    write_tables(c, chosen, table, where, plan)
+    spot_copy = pltpu.make_async_copy(where, spots, local2)
+    spot_copy.start()
 
     @pl.loop(1, PLANE)
     def _(i):
@@ -362,6 +368,25 @@
             def _(i):
                 most_copy(i).start()
 
+    spot_copy.wait()
+    for side in range(2):
+        for kv in range(2):
+            halo_copy(side, kv).wait()
+    for q in range(PARTS):
+
+        @pl.loop(1, PLANE)
+        def _(i):
+            plane_copy(q, i).wait_recv()
+
+    @pl.loop(0, HEADS_HERE)
+    def _(j):
+        cols = columns_of(j)
+        keys, far_keys = listed(spots, picked, halo, shared, key, 0, j)
+        w_near, w_far = softmax(seq, keys, far_keys, query[:, cols])
+        weights[j, : 6 * BLOCK] = w_near
+        weights[j, 6 * BLOCK :] = w_far
+        scatter(j, w_near.astype(BF16), w_far.astype(BF16), grad[:, cols], own, sides, both, terms)
+
     @pl.loop(1, 2 * DEPTH)
     def _(i):
         most_copy(i).wait()
@@ -384,17 +409,16 @@
 
             @pl.loop(1, PLANE)
             def _(i):
-                plane_copy(q, i).wait()
+                if q >= PARTS:
+                    plane_copy(q, i).wait_recv()
+                plane_copy(q, i).wait_send()
 
         for d in range(2):
             for t in range(ring_hops(q, d)):
                 ring_copy(q, d, t).wait_send()
-    for side in range(2):
-        for kv in range(2):
-            halo_copy(side, kv).wait()
-
-
-def fetch(c, ids, rand_peer, rand_local, key, value, collective_id):
+
+
+def fetch(c, ids, chosen, key, value, query, grad, collective_id):
     smem = pl.BlockSpec(memory_space=pltpu.SMEM)
     vmem = pl.BlockSpec(memory_space=pltpu.VMEM)
     part = jax.ShapeDtypeStruct((PLANE * c, ROWS, HEAD_DIM), BF16)
@@ -409,10 +433,15 @@
             jax.ShapeDtypeStruct((PLANE, 128), jnp.int32),
             jax.ShapeDtypeStruct((4, BLOCK, WIDTH), BF16),
             jax.ShapeDtypeStruct((CHUNKS * PLANE, ROWS, HEAD_DIM), BF16),
-        )
+            jax.ShapeDtypeStruct((HEADS_HERE, 9 * BLOCK, 128), F32),
+            jax.ShapeDtypeStruct((PARTS * ITEMS, ROWS, HEAD_DIM), F32),
+            jax.ShapeDtypeStruct((2 * PARTS * HEADS_HERE, ROWS, HEAD_DIM), BF16),
+            jax.ShapeDtypeStruct((PLANE * PARTS, ROWS, HEAD_DIM), BF16),
+        )
+        + (jax.ShapeDtypeStruct((PICKS, ROWS, HEAD_DIM), BF16),) * PARTS
         + (part,) * CHUNKS,
-        in_specs=[smem, vmem, vmem, vmem, vmem],
-        out_specs=(vmem,) * (6 + CHUNKS),
+        in_specs=[smem] + [vmem] * 5,
+        out_specs=(vmem,) * (10 + PARTS + CHUNKS),
         scratch_shapes=[pltpu.VMEM((DEPTH * ITEMS, ROWS, HEAD_DIM), BF16)] * CHUNKS
         + [pltpu.VMEM(part.shape, BF16)] * CHUNKS
         + [
@@ -422,8 +451,10 @@
             pltpu.VMEM((DEPTH, ROWS, HEAD_DIM), BF16),
             pltpu.VMEM((DEPTH, ROWS, HEAD_DIM), BF16),
             pltpu.SMEM((PLANE, 8, 128), jnp.int32),
+            pltpu.SMEM((PICKS, 128), jnp.int32),
             pltpu.VMEM((PLANE, 8, 128), jnp.int32),
             pltpu.VMEM((2 * DEPTH, 8, 128), jnp.int32),
+            dma(()),
             dma(()),
             dma((7 * (CHUNKS + 1),)),
             dma((7 * (CHUNKS + 1),)),
@@ -439,43 +470,79 @@
             dma((2 * DEPTH,)),
         ],
         compiler_params=pltpu.CompilerParams(
-            collective_id=collective_id, has_side_effects=True, vmem_limit_bytes=VMEM_BYTES
+            collective_id=collective_id, has_side_effects=True, vmem_limit_bytes=VMEM_FULL if c == FULL else VMEM_USUAL
         ),
         name=f"fetch_{c}",
-    )(ids, rand_peer, rand_local, key, value)
+    )(ids, chosen, key, value, query, grad)
 
 
 def dot(a, b, contract):
     return lax.dot_general(a, b, ((contract[0:1], contract[1:2]), ((), ())), preferred_element_type=F32)
 
 
-def back_kernel(c, ids, where, plan, order, first, ends, query, grad, key, value, halo, shared, *rest):
-    picked, rest = rest[:CHUNKS], rest[CHUNKS:]
-    outs, rest = rest[:4], rest[4:]
-    terms, rest = rest[:CHUNKS], rest[CHUNKS:]
-    out, rest = rest[:CHUNKS], rest[CHUNKS:]
-    arrived, rest = rest[:CHUNKS], rest[CHUNKS:]
-    totals, rest = rest[:CHUNKS], rest[CHUNKS:]
-    (
-        attended, grad_query, own, sides, both, weights,
-        zone_in, zone, tile_in, tile_total, relay, runs, zout, zin, beside, cross,
-        zsend, zrecv, psend, precv, gsend, grecv, hsend, hrecv, csend, crecv,
-    ) = rest
-    seq, z, p, head = position()
-
-    @pl.loop(1, PLANE)
-    def _(i):
-        signal(z * PLANE + lax.rem(p + i, PLANE), head)
-
-    @pl.loop(1, DEPTH)
-    def _(i):
-        signal(lax.rem(z + i, DEPTH) * PLANE + p, head)
-
-    for step in (1, PLANE * DEPTH - 1):
-        signal(lax.rem(seq + step, PLANE * DEPTH), head)
-    signal(seq, 1 - head)
-
-    scale = HEAD_DIM ** (-0.5)
+def columns_of(j):
+    return pl.ds(pl.multiple_of(j * HEAD_DIM, HEAD_DIM), HEAD_DIM)
+
+
+def listed(where, picked, halo, shared, rows, kv, j):
+    cols = columns_of(j)
+    close = [halo[kv, :, cols], rows[:, cols], halo[2 + kv, :, cols]]
+    for group in range(2):
+        for part in range(PARTS):
+            close.append(shared[(kv * PARTS + part) * PLANE + group * HEADS_HERE + j])
+    far = []
+    for b in range(BLOCKS_HERE):
+        pieces = []
+        for t in range(3):
+            at = where[t * ITEMS + b * HEADS_HERE + j, 0]
+            for part in range(PARTS):
+                pieces.append(picked[kv * PARTS + part][at])
+        far.append(jnp.concatenate(pieces, axis=0))
+    return jnp.concatenate(close, axis=0), far
+
+
+def first_block():
+    return lax.broadcasted_iota(jnp.int32, (3 * BLOCK, 128), 1) < BLOCK
+
+
+def products(close, far, other):
+    a = dot(close, other, (1, 1))
+    b = jnp.where(first_block(), dot(far[0], other, (1, 1)), dot(far[1], other, (1, 1)))
+    return a, b
+
+
+def gather(near_w, far_w, close, far):
+    total = dot(near_w, close, (0, 0))
+    top_rows = dot(far_w, far[0], (0, 0))
+    low_rows = dot(far_w, far[1], (0, 0))
+    return total + jnp.concatenate([top_rows[:BLOCK], low_rows[BLOCK:]], axis=0)
+
+
+def scatter(j, weight_near, weight_far, rows_here, own, sides, both, terms):
+    near_terms = dot(weight_near, rows_here, (1, 0))
+    zero = jnp.zeros_like(weight_far)
+    far_terms = (
+        dot(jnp.where(first_block(), weight_far, zero), rows_here, (1, 0)).astype(BF16),
+        dot(jnp.where(first_block(), zero, weight_far), rows_here, (1, 0)).astype(BF16),
+    )
+    for part in range(PARTS):
+
+        def piece(block):
+            start = block * BLOCK + part * ROWS
+            return near_terms[start : start + ROWS]
+
+        sides[part * HEADS_HERE + j] = piece(0).astype(BF16)
+        sides[(PARTS + part) * HEADS_HERE + j] = piece(3).astype(BF16)
+        for b in range(BLOCKS_HERE):
+            own[part * ITEMS + b * HEADS_HERE + j] = piece(1 + b)
+            for t in range(3):
+                start = t * BLOCK + part * ROWS
+                terms[part][t * ITEMS + b * HEADS_HERE + j] = far_terms[b][start : start + ROWS]
+        for group in range(2):
+            both[(group * HEADS_HERE + j) * PARTS + part] = piece(4 + group).astype(BF16)
+
+
+def softmax(seq, keys, far_keys, queries):
     near = 4 * BLOCK
     rows = lax.broadcasted_iota(jnp.int32, (near, 128), 0)
     lanes = lax.broadcasted_iota(jnp.int32, (near, 128), 1)
@@ -485,97 +552,65 @@
         | ((rows < BLOCK) & (seq == 0))
         | ((rows >= 3 * BLOCK) & (seq == PLANE * DEPTH - 1))
     )
-    pick_lanes = lax.broadcasted_iota(jnp.int32, (3 * BLOCK, 128), 1) < BLOCK
-
-    def columns_of(j):
-        return pl.ds(pl.multiple_of(j * HEAD_DIM, HEAD_DIM), HEAD_DIM)
-
-    def listed(kv, j):
-        cols = columns_of(j)
-        close = [halo[kv, :, cols], (key, value)[kv][:, cols], halo[2 + kv, :, cols]]
-        for group in range(2):
-            for part in range(PARTS):
-                close.append(shared[(kv * PARTS + part) * PLANE + group * HEADS_HERE + j])
-        far = []
-        for b in range(BLOCKS_HERE):
-            pieces = []
-            for t in range(3):
-                at = where[t * ITEMS + b * HEADS_HERE + j, 0]
-                for part in range(PARTS):
-                    pieces.append(picked[kv * PARTS + part][at])
-            far.append(jnp.concatenate(pieces, axis=0))
-        return jnp.concatenate(close, axis=0), far
-
-    def products(close, far, other):
-        a = dot(close, other, (1, 1))
-        b = jnp.where(pick_lanes, dot(far[0], other, (1, 1)), dot(far[1], other, (1, 1)))
-        return a, b
-
-    def gather(near_w, far_w, close, far):
-        total = dot(near_w, close, (0, 0))
-        top_rows = dot(far_w, far[0], (0, 0))
-        low_rows = dot(far_w, far[1], (0, 0))
-        return total + jnp.concatenate([top_rows[:BLOCK], low_rows[BLOCK:]], axis=0)
-
-    def scatter(kv, j, weight_near, weight_far, rows_here):
-        near_terms = dot(weight_near, rows_here, (1, 0))
-        zero = jnp.zeros_like(weight_far)
-        far_terms = (
-            dot(jnp.where(pick_lanes, weight_far, zero), rows_here, (1, 0)).astype(BF16),
-            dot(jnp.where(pick_lanes, zero, weight_far), rows_here, (1, 0)).astype(BF16),
-        )
-        for part in range(PARTS):
-            chunk = kv * PARTS + part
-
-            def piece(block):
-                start = block * BLOCK + part * ROWS
-                return near_terms[start : start + ROWS]
-
-            sides[chunk * HEADS_HERE + j] = piece(0).astype(BF16)
-            sides[(CHUNKS + chunk) * HEADS_HERE + j] = piece(3).astype(BF16)
-            for b in range(BLOCKS_HERE):
-                own[chunk * ITEMS + b * HEADS_HERE + j] = piece(1 + b)
-                for t in range(3):
-                    start = t * BLOCK + part * ROWS
-                    terms[chunk][t * ITEMS + b * HEADS_HERE + j] = far_terms[b][start : start + ROWS]
-            for group in range(2):
-                both[((kv * 2 + group) * HEADS_HERE + j) * PARTS + part] = piece(4 + group).astype(BF16)
-
-    def weigh(j):
-        cols = columns_of(j)
-        keys, far_keys = listed(0, j)
-        s_near, s_far = products(keys, far_keys, query[:, cols])
-        s_near = s_near * scale
-        s_far = s_far * scale
-        s_near = jnp.concatenate(
-            [jnp.where(hidden, -1e30, s_near[:near]), s_near[near:]], axis=0
-        )
-        top = jnp.maximum(
-            jnp.max(s_near, axis=0, keepdims=True), jnp.max(s_far, axis=0, keepdims=True)
-        )
-        w_near = jnp.exp(s_near - top)
-        w_far = jnp.exp(s_far - top)
-        total = jnp.sum(w_near, axis=0, keepdims=True) + jnp.sum(w_far, axis=0, keepdims=True)
-        inverse = 1.0 / total
-        w_near = w_near * inverse
-        w_far = w_far * inverse
-        weights[j, : 6 * BLOCK] = w_near
-        weights[j, 6 * BLOCK :] = w_far
-        scatter(1, j, w_near.astype(BF16), w_far.astype(BF16), grad[:, cols])
+    s_near, s_far = products(keys, far_keys, queries)
+    s_near = s_near * SCALE
+    s_far = s_far * SCALE
+    s_near = jnp.concatenate([jnp.where(hidden, -1e30, s_near[:near]), s_near[near:]], axis=0)
+    top = jnp.maximum(
+        jnp.max(s_near, axis=0, keepdims=True), jnp.max(s_far, axis=0, keepdims=True)
+    )
+    w_near = jnp.exp(s_near - top)
+    w_far = jnp.exp(s_far - top)
+    total = jnp.sum(w_near, axis=0, keepdims=True) + jnp.sum(w_far, axis=0, keepdims=True)
+    inverse = 1.0 / total
+    return w_near * inverse, w_far * inverse
+
+
+def back_kernel(
+    c, ids, where, plan, order, first, ends, query, grad, key, value, halo, shared, weights, own_v, sides_v, both_v, *rest
+):
+    terms_v, rest = rest[:PARTS], rest[PARTS:]
+    picked, rest = rest[:CHUNKS], rest[CHUNKS:]
+    outs, rest = rest[:4], rest[4:]
+    terms_k, rest = rest[:PARTS], rest[PARTS:]
+    out, rest = rest[:CHUNKS], rest[CHUNKS:]
+    arrived, rest = rest[:CHUNKS], rest[CHUNKS:]
+    totals, rest = rest[:CHUNKS], rest[CHUNKS:]
+    (
+        attended, grad_query, own_k, sides_k, both_k,
+        zone_in, zone, tile_in, extras, relay, runs, zout, zin, beside, cross,
+        zsend, zrecv, psend, precv, gsend, grecv, hsend, hrecv, csend, crecv,
+    ) = rest
+    seq, z, p, head = position()
+
+    @pl.loop(1, PLANE)
+    def _(i):
+        signal(z * PLANE + lax.rem(p + i, PLANE), head)
+
+    @pl.loop(1, DEPTH)
+    def _(i):
+        signal(lax.rem(z + i, DEPTH) * PLANE + p, head)
+
+    for step in (1, PLANE * DEPTH - 1):
+        signal(lax.rem(seq + step, PLANE * DEPTH), head)
+    signal(seq, 1 - head)
+
+    terms = terms_k + terms_v
+    own, sides, both = (own_k, own_v), (sides_k, sides_v), (both_k, both_v)
 
     def backward(j):
         cols = columns_of(j)
         q, g = query[:, cols], grad[:, cols]
-        keys, far_keys = listed(0, j)
-        values, far_values = listed(1, j)
+        keys, far_keys = listed(where, picked, halo, shared, key, 0, j)
+        values, far_values = listed(where, picked, halo, shared, value, 1, j)
         w_near, w_far = weights[j, : 6 * BLOCK], weights[j, 6 * BLOCK :]
         gw_near, gw_far = products(values, far_values, g)
         centre = jnp.sum(w_near * gw_near, axis=0, keepdims=True) + jnp.sum(
             w_far * gw_far, axis=0, keepdims=True
         )
-        d_near = (w_near * (gw_near - centre) * scale).astype(BF16)
-        d_far = (w_far * (gw_far - centre) * scale).astype(BF16)
-        scatter(0, j, d_near, d_far, q)
+        d_near = (w_near * (gw_near - centre) * SCALE).astype(BF16)
+        d_far = (w_far * (gw_far - centre) * SCALE).astype(BF16)
+        scatter(j, d_near, d_far, q, own_k, sides_k, both_k, terms_k)
         attended[:, cols] = gather(
             w_near.astype(BF16), w_far.astype(BF16), values, far_values
         ).astype(BF16)
@@ -602,7 +637,7 @@
         size = PARTS * HEADS_HERE
         other = lax.rem(seq + (PLANE * DEPTH - 1 if side == 0 else 1), PLANE * DEPTH)
         return remote(
-            sides.at[pl.ds((side * 2 + kv) * size, size)],
+            sides[kv].at[pl.ds(side * size, size)],
             beside.at[pl.ds(((1 - side) * 2 + kv) * size, size)],
             hsend.at[kv * 2 + side],
             hrecv.at[kv * 2 + side],
@@ -623,9 +658,9 @@
 
     def zone_copy(kv, i):
         other = lax.rem(z + i, DEPTH)
-        rows = pl.ds((kv * PLANE + other * 2) * PARTS, 2 * PARTS)
-        return remote(
-            both.at[rows],
+        rows = pl.ds(other * 2 * PARTS, 2 * PARTS)
+        return remote(
+            both[kv].at[rows],
             zone_in.at[pl.ds((kv * DEPTH + z) * 2 * PARTS, 2 * PARTS)],
             gsend.at[kv * DEPTH + i],
             grecv.at[kv * DEPTH + i],
@@ -648,7 +683,7 @@
         peer = lax.rem(p + i, PLANE)
         return remote(
             relay,
-            tile_total.at[p],
+            extras.at[z * PLANE + p],
             gsend.at[2 * DEPTH + PLANE + i],
             grecv.at[2 * DEPTH + PLANE + i],
             z * PLANE + peer,
@@ -669,7 +704,7 @@
             zone_copy(kv, i).wait_recv()
 
         size = 2 * PARTS
-        total = both[pl.ds((kv * PLANE + z * 2) * PARTS, size)].astype(F32)
+        total = both[kv][pl.ds(z * size, size)].astype(F32)
         for i in range(1, DEPTH):
             other = lax.rem(z + i, DEPTH)
             total = total + zone_in[pl.ds((kv * DEPTH + other) * size, size)].astype(F32)
@@ -693,11 +728,33 @@
             for i in range(1, PLANE):
                 total = total + tile_in[i].astype(F32)
             relay[...] = total.astype(BF16)
-            tile_total[p] = relay[...]
+            extras[z * PLANE + p] = relay[...]
 
             @pl.loop(1, PLANE)
             def _(i):
                 total_copy(i).start()
+
+    def extra_copy(kv, d, t):
+        step = 1 if d == 0 else DEPTH - 1
+        owner = lax.rem(z + t * (DEPTH - step), DEPTH)
+        rows = pl.ds(owner * PLANE + (1 - kv) * 2 * PARTS, 2 * PARTS)
+        slot = ring_slot(CHUNKS + kv, d, t)
+        return remote(
+            extras.at[rows],
+            extras.at[rows],
+            zsend.at[slot],
+            zrecv.at[slot],
+            lax.rem(z + step, DEPTH) * PLANE + p,
+            head,
+        )
+
+    def extra_step(kv, t):
+        for d in range(2):
+            hops = ring_hops(CHUNKS + kv, d)
+            if 0 < t <= hops:
+                extra_copy(kv, d, t - 1).wait_recv()
+            if t < hops:
+                extra_copy(kv, d, t).start()
 
     def total_wait(kv):
         @pl.loop(1, PLANE)
@@ -741,23 +798,10 @@
             return total
 
         lax.fori_loop(0, count, add, jnp.zeros((ROWS, HEAD_DIM), F32), unroll=8)
-        kv, part = q // PARTS, q % PARTS
-        if part == 0:
-            total_wait(kv)
-        extra = [
-            tile_total[(1 - kv) * 2 * PARTS + e * PARTS + part].astype(F32) for e in range(2)
-        ]
-        spots = []
-        for e in range(2):
-            _, column, item = global_place(ids, z * 2 + e)
-            spots.append(jnp.where(column == p, item, -1))
 
         @pl.loop(0, DEPTH * ITEMS, unroll=8)
         def _(i):
-            total = runs[ends[i]]
-            for e in range(2):
-                total = total + jnp.where(spots[e] == i, extra[e], 0.0)
-            totals[q][i] = total
+            totals[q][i] = runs[ends[i]]
 
     def ring_step(q, t):
         for d in range(2):
@@ -780,10 +824,15 @@
             for stays in range(2):
                 b = head if stays else 1 - head
                 item = b * HEADS_HERE + j
-                total = totals[q][z * ITEMS + item] + own[q * ITEMS + item]
+                total = totals[q][z * ITEMS + item] + own[kv][part * ITEMS + item]
                 total = total + beside[(b * CHUNKS + q) * HEADS_HERE + j].astype(F32)
                 for d in range(2):
                     total = total + zin[ring_slot(q, d, ring_hops(q, d) - 1), item].astype(F32)
+                for group in range(2):
+                    e = group * HEADS_HERE + j
+                    tile = (e // 2) * PLANE + (1 - kv) * 2 * PARTS + (e % 2) * PARTS + part
+                    mine_too = global_block(ids, e) == seq * BLOCKS_HERE + b
+                    total = total + jnp.where(mine_too, extras[tile].astype(F32), 0.0)
                 total = total.astype(BF16)
                 if stays:
                     cols = pl.ds(pl.multiple_of(head * WIDTH + j * HEAD_DIM, HEAD_DIM), HEAD_DIM)
@@ -792,52 +841,53 @@
                     cross[q, :, j * HEAD_DIM : (j + 1) * HEAD_DIM] = total
         cross_copy(q).start()
 
-    @pl.loop(0, HEADS_HERE)
-    def _(j):
-        weigh(j)
-
     runs[count] = jnp.zeros((ROWS, HEAD_DIM), F32)
     pl.semaphore_wait(pltpu.get_barrier_semaphore(), PLANE + DEPTH + 1)
     turn = list(range(PARTS, CHUNKS)) + list(range(PARTS))
     zone_start(1)
-    for side in range(2):
-        side_copy(1, side).start()
     spread(turn[0])
-    spread(turn[1])
 
     @pl.loop(0, HEADS_HERE)
     def _(j):
         backward(j)
 
+    zone_start(0)
+    spread(turn[1])
     zone_add(1)
     spread(turn[2])
-    zone_start(0)
-    for side in range(2):
-        side_copy(0, side).start()
     for k in range(2):
         result_copy(k).start()
         outs[k][:, mine] = (attended, grad_query)[k][pl.ds(pl.multiple_of(head * BLOCK, BLOCK), BLOCK)]
     for step in range(CHUNKS + 5):
         if 0 < step and step + 2 < CHUNKS:
             spread(turn[step + 2])
-        if step == 0:
+        if step == CHUNKS - 3:
+            for kv in (1, 0):
+                for side in range(2):
+                    side_copy(kv, side).start()
+        if step == 1:
             tile_add(1)
-        if step == 1:
             zone_add(0)
         if step == 3:
             tile_add(0)
+            total_wait(1)
+        if step == 5:
+            total_wait(0)
+        for kv in range(2):
+            if 0 <= step - (5 - 2 * kv) <= 4:
+                extra_step(kv, step - (5 - 2 * kv))
         for t in range(3, 0, -1):
             if 0 <= step - t < CHUNKS:
                 ring_step(turn[step - t], t)
         if step < CHUNKS:
             collect(turn[step])
             ring_step(turn[step], 0)
-        if 0 <= step - 4 < CHUNKS:
-            q = turn[step - 4]
-            if q % PARTS == 0:
-                for side in range(2):
-                    side_copy(q // PARTS, side).wait()
-            finish(q)
+        for n, q in enumerate(turn):
+            if step == (9, 9, 9, 10, 10, 10, 11, 11)[n]:
+                if n % PARTS == 0:
+                    for side in range(2):
+                        side_copy(q // PARTS, side).wait()
+                finish(q)
     for kv in range(2):
 
         @pl.loop(1, DEPTH)
@@ -854,6 +904,10 @@
     def _(i):
         total_copy(i).wait_send()
 
+    for kv in range(2):
+        for d in range(2):
+            for t in range(ring_hops(CHUNKS + kv, d)):
+                extra_copy(kv, d, t).wait_send()
     for q in range(CHUNKS):
 
         @pl.loop(1, PLANE)
@@ -868,7 +922,7 @@
         result_copy(k).wait()
 
 
-def back(c, scalars, arrays, picked, collective_id):
+def back(c, scalars, arrays, tiles, collective_id):
     smem = pl.BlockSpec(memory_space=pltpu.SMEM)
     vmem = pl.BlockSpec(memory_space=pltpu.VMEM)
     dma = pltpu.SemaphoreType.DMA
@@ -878,30 +932,29 @@
     return pl.pallas_call(
         functools.partial(back_kernel, c),
         out_shape=(jax.ShapeDtypeStruct((BLOCK, 2 * WIDTH), BF16),) * 4,
-        in_specs=[smem] * len(scalars) + [vmem] * (len(arrays) + CHUNKS),
+        in_specs=[smem] * len(scalars) + [vmem] * (len(arrays) + len(tiles)),
         out_specs=(vmem,) * 4,
-        scratch_shapes=[vm((PICKS,) + tile, BF16)] * CHUNKS
+        scratch_shapes=[vm((PICKS,) + tile, BF16)] * PARTS
         + [vm(part, BF16)] * (2 * CHUNKS)
         + [vm((DEPTH * ITEMS,) + tile, F32)] * CHUNKS
         + [
             vm((BLOCKS_HERE * BLOCK, WIDTH), BF16),
             vm((BLOCKS_HERE * BLOCK, WIDTH), BF16),
-            vm((CHUNKS * ITEMS,) + tile, F32),
-            vm((2 * CHUNKS * HEADS_HERE,) + tile, BF16),
-            vm((CHUNKS * PLANE,) + tile, BF16),
-            vm((HEADS_HERE, 9 * BLOCK, 128), F32),
+            vm((PARTS * ITEMS,) + tile, F32),
+            vm((2 * PARTS * HEADS_HERE,) + tile, BF16),
+            vm((PLANE * PARTS,) + tile, BF16),
             vm((2 * DEPTH * 2 * PARTS,) + tile, BF16),
             vm((2 * 2 * PARTS,) + tile, BF16),
             vm((PLANE,) + tile, BF16),
-            vm((PLANE,) + tile, BF16),
+            vm((DEPTH * PLANE,) + tile, BF16),
             vm(tile, BF16),
             vm((PLANE * c + 1,) + tile, F32),
             vm((7 * CHUNKS, ITEMS) + tile, BF16),
             vm((7 * CHUNKS, ITEMS) + tile, BF16),
             vm((2 * CHUNKS * HEADS_HERE,) + tile, BF16),
             vm((CHUNKS, ROWS, WIDTH), BF16),
-            dma((7 * CHUNKS,)),
-            dma((7 * CHUNKS,)),
+            dma((7 * (CHUNKS + 2),)),
+            dma((7 * (CHUNKS + 2),)),
             dma((CHUNKS * PLANE,)),
             dma((CHUNKS * PLANE,)),
             dma((2 * DEPTH + 2 * PLANE,)),
@@ -912,10 +965,10 @@
             dma((2 + CHUNKS,)),
         ],
         compiler_params=pltpu.CompilerParams(
-            collective_id=collective_id, has_side_effects=True, vmem_limit_bytes=VMEM_BYTES
+            collective_id=collective_id, has_side_effects=True, vmem_limit_bytes=VMEM_FULL if c == FULL else VMEM_USUAL
         ),
         name=f"back_{c}",
-    )(*scalars, *arrays, *picked)
+    )(*scalars, *arrays, *tiles)
 
 
 def on_device(
@@ -924,11 +977,11 @@
     none = DEPTH * ITEMS
     all_items = jnp.arange(none, dtype=jnp.int32)
 
-    def go(c, collective_id, peers, spots, key, value):
-        return fetch(c, global_ids, peers, spots, key, value, collective_id)
+    def go(c, collective_id, query, key, value, grad, chosen):
+        return fetch(c, global_ids, chosen, key, value, query, grad, collective_id)
 
     def finish(c, collective_id, query, key, value, grad, fetched):
-        got, _, where, plan, halo, shared, *picked = fetched
+        got, _, where, plan, halo, shared, weights, own, sides, both, *tiles = fetched
         count = PLANE * c
         keys = got[:, 0, 2 * LANES : 2 * LANES + c].reshape(count)
         at = jnp.arange(count, dtype=jnp.int32)
@@ -946,22 +999,25 @@
         return back(
             c,
             (global_ids, where, plan, order, first, ends),
-            (query, grad, key, value, halo, shared),
-            picked,
+            (query, grad, key, value, halo, shared, weights, own, sides, both),
+            tiles,
             collective_id,
         )
 
-    def usual(query, key, value, grad, peers, spots, *fetched):
-        return finish(USUAL, 1, query, key, value, grad, fetched)
-
-    def crowded(query, key, value, grad, peers, spots, *fetched):
-        return finish(FULL, 3, query, key, value, grad, go(FULL, 2, peers, spots, key, value))
-
-    fetched = go(USUAL, 0, rand_peer, rand_local, key_vectors, value_vectors)
-    return lax.cond(
-        fetched[1][0, LANES] > USUAL, crowded, usual,
-        query_vectors, key_vectors, value_vectors, cotangent, rand_peer, rand_local, *fetched,
-    )
+    def few(*args):
+        return finish(FEW, 4, *args[:4], args[5:])
+
+    def usual(*args):
+        return finish(USUAL, 1, *args[:4], args[5:])
+
+    def crowded(*args):
+        return finish(FULL, 3, *args[:4], go(FULL, 2, *args[:5]))
+
+    args = (query_vectors, key_vectors, value_vectors, cotangent, rand_peer * BLOCKS_HERE + rand_local)
+    fetched = go(USUAL, 0, *args)
+    peak = fetched[1][0, LANES]
+    level = (peak > FEW).astype(jnp.int32) + (peak > USUAL).astype(jnp.int32)
+    return lax.switch(level, (few, usual, crowded), *args, *fetched)
 
 
 def solution(mesh):

time: 193 us -> 197 us (1.021)
  Pallas kernels: 182 us -> 184 us
    unnamed x22 -> x6, local copies, waits for them, and re-layouts: 5.87 us -> 8.21 us
where the time goes in v4:
time: 197 us; the launch traced here: 196 us
  Pallas kernels  184 us (93%)
  local copies, waits for them, and re-layouts  8.97 us (5%)
  between operations  1.97 us (1%)
    pallas_call x1, Pallas kernels, back(): pl.pallas_call(functools.partial(back_kernel, c), out_shape=(jax.ShapeDty...  99 us
    pallas_call x1, Pallas kernels, fetch(): pl.pallas_call(functools.partial(fetch_kernel, c), out_shape=(rows, jax.S...  85.1 us
    unnamed x6, local copies, waits for them, and re-layouts  8.21 us

profile of v4, /device:TPU:1, one launch (start us, length us, event | category | flops | bytes accessed | tf_op | source)
XLA Modules:
  0.0 196.1 jit_solution(1714463858843596211)
XLA Ops:
  0.6 0.8 copy.31
  1.4 0.8 copy.32
  2.2 85.1 %fetch_8.1 = (s32[16,8,128]{2,1,0:T(8,128)S(1)}, s32[8,128]{1,0:T(8,128)S(1)}, s32[48,128]{1,0:T(8,128)S(1)}, s32[16,128]{1,0:T(8,128)S(1)}, bf16[4,64,1024]{2,1...) custom-call(s32[2]{0:T(128)} %ids.1, ...), custom_call_target="tpu_custom_call" | custom-call | tf_op jit(solution)/shard_map/fetch_8/pallas_call | solution.py:427
  87.3 0.6 slice.12
  89.2 100.2 %conditional.1 = ((bf16[64,2048]{1,0:T(8,128)(2,1)}, bf16[64,2048]{1,0:T(8,128)(2,1)}, bf16[64,2048]{1,0:T(8,128)(2,1)}, bf16[64,2048]{1,0:T(8,128)(2,1)})) conditional(s32[]{:T(128)} %bitcast, (s32[16,8,128]{2,1,0:T(8,128)S(1)}, s32[128]{0:T(128)S(1)}, s32[128]{0:T(128)S(1)}, s32[2]{0:T(128)}, s32[48,128]{1,0:T(8,128)S(1)}, ...), branch_computations={%region_0.7_spmd, %region_7.14_spmd, %region_14.21_spmd} | conditional | flops 1277184 | bytes 139720 | solution.py:1020
  89.2 0.1 slice.14
  89.3 0.1 lt.64
  89.4 0.2 convert_reduce_fusion.2
  89.6 0.2 compare_reduce_fusion.1
  89.8 0.1 select_reduce_fusion.2
  89.9 99.0 %back_8.1 = (bf16[64,2048]{1,0:T(8,128)(2,1)}, bf16[64,2048]{1,0:T(8,128)(2,1)}, bf16[64,2048]{1,0:T(8,128)(2,1)}, bf16[64,2048]{1,0:T(8,128)(2,1)}) custom-call(s32[2]{0:T(128)} %get-tuple-element.153.ids, s32[48,128]{1,0:T(8,128)S(1)} %get-tuple-element.154.where, s32[16,128]{1,0:T(8,128)S(1)} %get-tuple-element.155.plan, ...), custom_call_target="tpu_custom_call" | custom-call | tf_op jit(solution)/shard_map/cond/branch_1_fun/back_8/pallas_call | solution.py:932
  189.4 1.7 copy.51
  191.1 1.7 copy.52
  192.7 1.7 copy.53
  194.4 1.7 copy.54
  (6 shorter events, 0.0 us)

commit v5 on v3

--- a/solution.py
+++ b/solution.py
@@ -458,7 +458,7 @@
     totals, rest = rest[:CHUNKS], rest[CHUNKS:]
     (
         attended, grad_query, own, sides, both, weights,
-        zone_in, zone, tile_in, tile_total, relay, runs, zout, zin, beside, cross,
+        zone_in, zone, tile_in, extras, relay, runs, zout, zin, beside, cross,
         zsend, zrecv, psend, precv, gsend, grecv, hsend, hrecv, csend, crecv,
     ) = rest
     seq, z, p, head = position()
@@ -648,7 +648,7 @@
         peer = lax.rem(p + i, PLANE)
         return remote(
             relay,
-            tile_total.at[p],
+            extras.at[z * PLANE + p],
             gsend.at[2 * DEPTH + PLANE + i],
             grecv.at[2 * DEPTH + PLANE + i],
             z * PLANE + peer,
@@ -693,11 +693,33 @@
             for i in range(1, PLANE):
                 total = total + tile_in[i].astype(F32)
             relay[...] = total.astype(BF16)
-            tile_total[p] = relay[...]
+            extras[z * PLANE + p] = relay[...]
 
             @pl.loop(1, PLANE)
             def _(i):
                 total_copy(i).start()
+
+    def extra_copy(kv, d, t):
+        step = 1 if d == 0 else DEPTH - 1
+        owner = lax.rem(z + t * (DEPTH - step), DEPTH)
+        rows = pl.ds(owner * PLANE + (1 - kv) * 2 * PARTS, 2 * PARTS)
+        slot = ring_slot(CHUNKS + kv, d, t)
+        return remote(
+            extras.at[rows],
+            extras.at[rows],
+            zsend.at[slot],
+            zrecv.at[slot],
+            lax.rem(z + step, DEPTH) * PLANE + p,
+            head,
+        )
+
+    def extra_step(kv, t):
+        for d in range(2):
+            hops = ring_hops(CHUNKS + kv, d)
+            if 0 < t <= hops:
+                extra_copy(kv, d, t - 1).wait_recv()
+            if t < hops:
+                extra_copy(kv, d, t).start()
 
     def total_wait(kv):
         @pl.loop(1, PLANE)
@@ -741,23 +763,10 @@
             return total
 
         lax.fori_loop(0, count, add, jnp.zeros((ROWS, HEAD_DIM), F32), unroll=8)
-        kv, part = q // PARTS, q % PARTS
-        if part == 0:
-            total_wait(kv)
-        extra = [
-            tile_total[(1 - kv) * 2 * PARTS + e * PARTS + part].astype(F32) for e in range(2)
-        ]
-        spots = []
-        for e in range(2):
-            _, column, item = global_place(ids, z * 2 + e)
-            spots.append(jnp.where(column == p, item, -1))
 
         @pl.loop(0, DEPTH * ITEMS, unroll=8)
         def _(i):
-            total = runs[ends[i]]
-            for e in range(2):
-                total = total + jnp.where(spots[e] == i, extra[e], 0.0)
-            totals[q][i] = total
+            totals[q][i] = runs[ends[i]]
 
     def ring_step(q, t):
         for d in range(2):
@@ -784,6 +793,11 @@
                 total = total + beside[(b * CHUNKS + q) * HEADS_HERE + j].astype(F32)
                 for d in range(2):
                     total = total + zin[ring_slot(q, d, ring_hops(q, d) - 1), item].astype(F32)
+                for group in range(2):
+                    e = group * HEADS_HERE + j
+                    tile = (e // 2) * PLANE + (1 - kv) * 2 * PARTS + (e % 2) * PARTS + part
+                    mine_too = global_block(ids, e) == seq * BLOCKS_HERE + b
+                    total = total + jnp.where(mine_too, extras[tile].astype(F32), 0.0)
                 total = total.astype(BF16)
                 if stays:
                     cols = pl.ds(pl.multiple_of(head * WIDTH + j * HEAD_DIM, HEAD_DIM), HEAD_DIM)
@@ -800,44 +814,49 @@
     pl.semaphore_wait(pltpu.get_barrier_semaphore(), PLANE + DEPTH + 1)
     turn = list(range(PARTS, CHUNKS)) + list(range(PARTS))
     zone_start(1)
-    for side in range(2):
-        side_copy(1, side).start()
     spread(turn[0])
-    spread(turn[1])
 
     @pl.loop(0, HEADS_HERE)
     def _(j):
         backward(j)
 
+    zone_start(0)
+    spread(turn[1])
     zone_add(1)
     spread(turn[2])
-    zone_start(0)
-    for side in range(2):
-        side_copy(0, side).start()
     for k in range(2):
         result_copy(k).start()
         outs[k][:, mine] = (attended, grad_query)[k][pl.ds(pl.multiple_of(head * BLOCK, BLOCK), BLOCK)]
     for step in range(CHUNKS + 5):
         if 0 < step and step + 2 < CHUNKS:
             spread(turn[step + 2])
-        if step == 0:
+        if step == CHUNKS - 3:
+            for kv in (1, 0):
+                for side in range(2):
+                    side_copy(kv, side).start()
+        if step == 1:
             tile_add(1)
-        if step == 1:
             zone_add(0)
         if step == 3:
             tile_add(0)
+            total_wait(1)
+        if step == 5:
+            total_wait(0)
+        for kv in range(2):
+            if 0 <= step - (5 - 2 * kv) <= 4:
+                extra_step(kv, step - (5 - 2 * kv))
         for t in range(3, 0, -1):
             if 0 <= step - t < CHUNKS:
                 ring_step(turn[step - t], t)
         if step < CHUNKS:
             collect(turn[step])
             ring_step(turn[step], 0)
-        if 0 <= step - 4 < CHUNKS:
-            q = turn[step - 4]
-            if q % PARTS == 0:
-                for side in range(2):
-                    side_copy(q // PARTS, side).wait()
-            finish(q)
+        for n, q in enumerate(turn):
+            if step == (9, 9, 9, 10, 10, 10, 11, 11)[n]:
+                if n % PARTS == 0:
+                    for side in range(2):
+                        side_copy(q // PARTS, side).wait()
+                finish(q)
     for kv in range(2):
 
         @pl.loop(1, DEPTH)
@@ -854,6 +873,10 @@
     def _(i):
         total_copy(i).wait_send()
 
+    for kv in range(2):
+        for d in range(2):
+            for t in range(ring_hops(CHUNKS + kv, d)):
+                extra_copy(kv, d, t).wait_send()
     for q in range(CHUNKS):
 
         @pl.loop(1, PLANE)
@@ -893,15 +916,15 @@
             vm((2 * DEPTH * 2 * PARTS,) + tile, BF16),
             vm((2 * 2 * PARTS,) + tile, BF16),
             vm((PLANE,) + tile, BF16),
-            vm((PLANE,) + tile, BF16),
+            vm((DEPTH * PLANE,) + tile, BF16),
             vm(tile, BF16),
             vm((PLANE * c + 1,) + tile, F32),
             vm((7 * CHUNKS, ITEMS) + tile, BF16),
             vm((7 * CHUNKS, ITEMS) + tile, BF16),
             vm((2 * CHUNKS * HEADS_HERE,) + tile, BF16),
             vm((CHUNKS, ROWS, WIDTH), BF16),
-            dma((7 * CHUNKS,)),
-            dma((7 * CHUNKS,)),
+            dma((7 * (CHUNKS + 2),)),
+            dma((7 * (CHUNKS + 2),)),
             dma((CHUNKS * PLANE,)),
             dma((CHUNKS * PLANE,)),
             dma((2 * DEPTH + 2 * PLANE,)),

time: 193 us -> 193 us (level)
  no operation moved by 1% of the time
where the time goes in v5:
time: 193 us; the launch traced here: 192 us
  Pallas kernels  182 us (94%)
  local copies, waits for them, and re-layouts  7.31 us (4%)
    pallas_call x1, Pallas kernels, back(): pl.pallas_call(functools.partial(back_kernel, c), out_shape=(jax.ShapeDty...  97.9 us
    pallas_call x1, Pallas kernels, fetch(): pl.pallas_call(functools.partial(fetch_kernel, c), out_shape=(rows, jax.S...  84 us
    unnamed x22, local copies, waits for them, and re-layouts  5.87 us

profile of v5, /device:TPU:1, one launch (start us, length us, event | category | flops | bytes accessed | tf_op | source)
XLA Modules:
  0.0 192.3 jit_solution(11486447865067958526)
XLA Ops:
  0.6 0.0 copy-start.7
  0.7 0.7 copy-done.7
  1.3 0.0 copy-start.8
  1.3 0.7 copy.29.rand_peer
  2.0 0.0 copy-done.8
  2.0 0.0 copy-start.9
  2.0 0.7 copy.30.rand_local
  2.7 0.0 copy-done.9
  2.7 0.0 copy-start
  2.7 0.0 copy-start.1
  2.7 84.0 %fetch_8.1 = (s32[16,8,128]{2,1,0:T(8,128)S(1)}, s32[8,128]{1,0:T(8,128)}, s32[48,128]{1,0:T(8,128)S(1)}, s32[16,128]{1,0:T(8,128)S(1)}, bf16[4,64,1024]{2,1,0:T...) custom-call(s32[2]{0:T(128)S(1)} %copy-done.9, ...), custom_call_target="tpu_custom_call" | custom-call | tf_op jit(solution)/shard_map/fetch_8/pallas_call | solution.py:403
  86.7 1.3 slice.9
  88.6 0.0 copy-done
  88.7 0.0 copy-done.1
  88.7 99.8 %conditional.1 = ((bf16[64,2048]{1,0:T(8,128)(2,1)S(1)}, bf16[64,2048]{1,0:T(8,128)(2,1)}, bf16[64,2048]{1,0:T(8,128)(2,1)}, bf16[64,2048]{1,0:T(8,128)(2,1)})) conditional(s32[]{:T(128)} %bitcast, (s32[16,8,128]{2,1,0:T(8,128)S(1)}, s32[128]{0:T(128)S(1)}, s32[128]{0:T(128)S(1)}, s32[2]{0:T(128)S(1)}, s32[48,128]{1,0:T(8,128)S(1)}, ...), branch_computations={%region_0.7_spmd, %region_7.14_spmd} | conditional | flops 1277184 | bytes 2114112 | solution.py:984
  88.7 0.1 slice.10
  88.8 0.1 lt.5
  88.9 0.2 convert_reduce_fusion
  89.1 0.2 compare_reduce_fusion
  89.2 0.5 add_select_fusion.ends
  89.8 0.6 select_reduce_fusion
  90.4 97.9 %back_8.1 = (bf16[64,2048]{1,0:T(8,128)(2,1)S(1)}, bf16[64,2048]{1,0:T(8,128)(2,1)}, bf16[64,2048]{1,0:T(8,128)(2,1)}, bf16[64,2048]{1,0:T(8,128)(2,1)}) custom-call(s32[2]{0:T(128)S(1)} %get-tuple-element.44.ids, s32[48,128]{1,0:T(8,128)S(1)} %get-tuple-element.45.where, s32[16,128]{1,0:T(8,128)S(1)} %get-tuple-element.58.plan, ...), custom_call_target="tpu_custom_call" | custom-call | tf_op jit(solution)/shard_map/cond/branch_0_fun/back_8/pallas_call | solution.py:901
  188.5 0.0 copy-start.4
  188.5 0.7 copy.46
  189.2 0.3 copy-done.4
  189.5 0.0 copy-start.5
  189.5 0.7 copy.47
  190.2 0.3 copy-done.5
  190.6 0.0 copy-start.6
  190.6 0.7 copy.48
  191.3 0.3 copy-done.6
  191.6 0.7 copy.49
  (4 shorter events, 0.0 us)
Async XLA Ops:
  0.6 0.7 copy-start.7
  1.3 0.7 copy-start.8
  2.0 0.7 copy-start.9
  2.7 85.9 %copy-start = (bf16[128,1024]{1,0:T(8,128)(2,1)S(1)}, bf16[128,1024]{1,0:T(8,128)(2,1)}, u32[]{:S(2)}) copy-start(bf16[128,1024]{1,0:T(8,128)(2,1)} %key.1) | copy-start | bytes 786436
  2.7 86.0 %copy-start.1 = (bf16[128,1024]{1,0:T(8,128)(2,1)S(1)}, bf16[128,1024]{1,0:T(8,128)(2,1)}, u32[]{:S(2)}) copy-start(bf16[128,1024]{1,0:T(8,128)(2,1)} %value.1) | copy-start | bytes 786436
  188.5 1.0 copy-start.4
  189.5 1.0 copy-start.5
  190.6 1.0 copy-start.6
